TPU v7x, 512 devices: a whole 4x8x8 slice. The times are simulated.
512 devices in a mesh: dp: 64 (over y, x, core), tensor: 8 (over z).
Axes of the slice: x: 4, y: 8, z: 8, core: 2. Of those that a mesh axis runs over, the one named last changes fastest.
Arguments:
- grad_terms: bfloat16 [8, 8192, 12288], P('tensor', 'dp'), may hold values from -24 to 24
- acts: bfloat16 [8192, 12288], P('dp', 'tensor'), may hold values from -24 to 24
- kept: int32 [64, 8, 32], P('dp', 'tensor'), may hold values from 0 to 1151, as said below
- starts: int32 [8, 64], P('tensor'), may hold values from 0 to 1148, as said below
Outputs:
- normed: bfloat16 [64, 8, 32, 128, 128], P('dp', 'tensor')
Inputs may be any that keep to these rules, and one draw needn't show every extreme that they name: kept[r, t] lists distinct blocks of rank t's gradient, block b covering rows 128 * (b // 96) and columns 128 * (b % 96) of it. A replica keeps either no block or exactly 2 blocks of each owner's region. At most 4 distinct blocks of one region are kept by all replicas together. Every region holds a kept block, and some owner's region has 2 blocks kept by every replica. starts[t, 0] is 0; starts rise, and each region, from starts[t, o] up to the next start (or 1152), holds 4 or more blocks.
All inputs are finite; a program needn't handle non-finite values.
Results may differ from a plain program's by a relative error of at most 0.022.
Values may be sent and summed in bfloat16 or wider, within the bound.
A program may use at most 64 MiB of HBM per device.

v0:
```python
import jax
import jax.numpy as jnp
from jax import lax
from jax.sharding import PartitionSpec as P

BLOCK = 128
SLOTS = 2


epsilon = 1e-06


def shards(grad_terms, acts, kept, starts):
    tok_rows = acts.shape[0]
    features = grad_terms.shape[2]
    col_blocks = features // BLOCK
    owners = lax.axis_size("dp")
    slots_all = owners * SLOTS
    chosen = kept[0, 0]
    row_block = chosen // col_blocks
    col_block = chosen % col_blocks
    sel_a = jnp.take(acts.reshape(tok_rows, acts.shape[1] // BLOCK, BLOCK), row_block, axis=1)
    summed = lax.psum(grad_terms[0].astype(jnp.float32).astype(jnp.bfloat16), "tensor")
    sel_g = jnp.take(summed.reshape(tok_rows, col_blocks, BLOCK), col_block, axis=1)
    bounds = starts[0]
    owner_of = jnp.sum((bounds[None, :] <= chosen[:, None]).astype(jnp.int32), axis=1) - 1
    position = jnp.arange(chosen.shape[0], dtype=jnp.int32)
    earlier = (owner_of[:, None] == owner_of[None, :]) & (position[None, :] < position[:, None])
    slot_of = owner_of * SLOTS + jnp.sum(earlier.astype(jnp.int32), axis=1)
    matches = jnp.arange(slots_all, dtype=jnp.int32)[:, None] == slot_of[None, :]
    filled = jnp.any(matches, axis=1)
    source = jnp.sum(jnp.where(matches, position[None, :], 0), axis=1)
    slot_idx = jnp.where(filled, jnp.take(chosen, source), -1)
    operands = jnp.concatenate([sel_a, sel_g], axis=2)
    packed = jnp.where(
        filled[None, :, None], jnp.take(operands, source, axis=1), jnp.zeros((), jnp.bfloat16)
    )
    packed = packed.reshape(tok_rows, owners, SLOTS, 2 * BLOCK)
    arrived, arrived_ids = (
        lax.all_to_all(packed, "dp", split_axis=1, concat_axis=1, tiled=True),
        lax.all_to_all(
            slot_idx.reshape(1, owners, SLOTS), "dp", split_axis=1, concat_axis=1, tiled=True
        ),
    )
    unpacked = arrived.reshape(tok_rows, slots_all, 2 * BLOCK)
    computed = jnp.einsum(
        "tmr,tmc->mrc",
        unpacked[:, :, :BLOCK],
        unpacked[:, :, BLOCK:],
        preferred_element_type=jnp.float32,
    )
    received = lax.optimization_barrier(computed.astype(jnp.bfloat16)).astype(jnp.float32)
    received = received.reshape(slots_all, BLOCK * BLOCK)
    slot_ids = arrived_ids.reshape(slots_all)
    in_use = slot_ids >= 0
    matching = ((slot_ids[:, None] == slot_ids[None, :]) & in_use[:, None]).astype(jnp.float32)
    totals = jnp.dot(matching, received, precision=lax.Precision.HIGHEST)
    copies = jnp.maximum(jnp.sum(matching, axis=1), 1.0)
    share_w = jnp.where(in_use, 1.0 / copies, 0.0)
    energy = jnp.sum(share_w * jnp.sum(totals * totals, axis=1))
    distinct = jnp.sum(share_w)
    mean_sq = energy / (distinct * (BLOCK * BLOCK))
    normed = (totals * lax.rsqrt(mean_sq + epsilon)).astype(jnp.bfloat16)
    normed = normed.reshape(owners, SLOTS, BLOCK, BLOCK)
    returned = lax.all_to_all(normed, "dp", split_axis=0, concat_axis=0, tiled=True)
    result = jnp.take(returned.reshape(slots_all, BLOCK, BLOCK), slot_of, axis=0)
    return result.reshape(1, 1, chosen.shape[0], BLOCK, BLOCK)


def solution(mesh):
    placed = (
        P("tensor", "dp", None),
        P("dp", "tensor"),
        P("dp", "tensor", None),
        P("tensor", None),
    )
    return jax.shard_map(
        shards,
        mesh=mesh,
        in_specs=placed,
        out_specs=P("dp", "tensor", None, None, None),
        check_vma=False,
    )
```

profile of v0, /device:TPU:1, one launch (start us, length us, event | category | flops | bytes accessed | tf_op | source)
XLA Modules:
  0.0 463.5 jit_solution(15730210962986900134)
XLA Ops:
  6.5 3.6 copy.25
  10.1 2.8 copy.26
  13.0 0.2 convert_reduce_fusion.2
  13.2 0.2 convert_reduce_fusion.1
  13.4 0.6 compare_and_fusion.5
  14.2 0.3 copy-done.3
  14.7 1.2 gather_fusion
  16.1 0.6 select_select_fusion.1
  16.7 11.8 %all-to-all-start = ((s32[1,64,2]{2,0,1:T(1,128)}), s32[1,64,2]{2,0,1:T(1,128)}, u32[]{:S(2)}, u32[]{:S(2)}) async-start(s32[1,64,2]{2,0,1:T(1,128)} %bitcast.4), calls=%async_computation | async-start | bytes 65536 | tf_op jit(solution)/shard_map/all_to_all | solution.py:41
  28.9 0.2 copy.23
  29.1 0.3 copy.24
  29.4 0.7 gather_fusion.1
  30.2 0.2 select_bitcast_fusion.1
  30.4 85.5 %all-reduce.2.cloned.1.call-done = bf16[128,96,128]{2,0,1:T(8,128)(2,1)} async-done(((bf16[128,96,128]{2,0,1:T(8,128)(2,1)}), bf16[128,96,128]{2,0,1:T(8,128)(2,1)}) %all-reduce.2.cloned.1.call-update) | async-done | bytes 3145744 | tf_op jit(solution)/shard_map/psum | solution.py:23
  115.9 2.6 gather_fusion.2
  118.7 0.2 pad_maximum_fusion
  119.0 6.4 %gather_fusion.3 = bf16[128,128,256]{2,1,0:T(8,128)(2,1)} fusion(bf16[128,32,256]{2,0,1:T(8,128)(2,1)S(1)} %pad_maximum_fusion, s32[1024]{0:T(1024)S(1)} %pad_clamp_fusion.3), kind=kCustom, calls=%fused_computation.3 | custom fusion | bytes 16777728 | tf_op jit(solution)/shard_map/jit(_take)/gather | solution.py:36
  125.4 7.4 %select_select_fusion = bf16[128,64,2,256]{3,0,2,1:T(8,128)(2,1)} fusion(bf16[128,64,2,256]{3,0,2,1:T(8,128)(2,1)} %bitcast.59, pred[64,2]{1,0:T(8,128)(4,1)S(1)} %compare_and_fusion.2, pred[64,2]{1,0:T(8,128)(4,1)S(1)} %broadcast_in_dim.92), kind=kLoop, calls=%fused_computation.7 | loop fusion | flops 8388608 | bytes 16777472 | tf_op jit(solution)/shard_map/jit(_where)/select_n | solution.py:35
  132.8 10.7 %all-to-all-start.1 = ((bf16[128,64,2,256]{3,0,2,1:T(8,128)(2,1)}), bf16[128,64,2,256]{3,0,2,1:T(8,128)(2,1)}, u32[]{:S(2)}, u32[]{:S(2)}) async-start(bf16[128,64,2,256]{3,0,2,1:T(8,128)(2,1)} %select_select_fusion), calls=%async_computation.1 | async-start | bytes 16777216 | tf_op jit(solution)/shard_map/all_to_all | solution.py:40
  143.5 0.5 broadcast.354
  144.0 1.5 reduce.5
  145.7 0.2 convert_reduce_fusion
  146.0 180.0 %all-to-all-done.1 = bf16[128,64,2,256]{3,0,2,1:T(8,128)(2,1)} async-done(((bf16[128,64,2,256]{3,0,2,1:T(8,128)(2,1)}), bf16[128,64,2,256]{3,0,2,1:T(8,128)(2,1)}, u32[]{:S(2)}, u32[]{:S(2)}) %all-to-all-start.1) | async-done | bytes 8388640 | tf_op jit(solution)/shard_map/all_to_all | solution.py:40
  326.0 5.0 %fusion.7 = bf16[128,128,128]{2,1,0:T(8,128)(2,1)S(1)} fusion(bf16[128,128,256]{2,0,1:T(8,128)(2,1)} %bitcast.16), kind=kOutput, calls=%fused_computation.15 | convolution fusion | flops 538968064 | bytes 12582912 | tf_op jit(solution)/shard_map/tmr,tmc->mrc/dot_general | solution.py:46
  331.0 6.5 %multiply_reduce_fusion = (f32[128]{0:T(128)S(1)}, f32[128,16384]{1,0:T(8,128)}) fusion(bf16[16,8,128,128]{3,2,1,0:T(8,128)(2,1)S(1)} %bitcast.60, s32[128]{0:T(128)S(1)} %eq.49, pred[128]{0:T(512)(128)(4,1)S(1)} %broadcast_compare_fusion), kind=kOutput, calls=%fused_computation.6 | convolution fusion | flops 541097856 | bytes 12584064 | tf_op jit(solution)/shard_map/dot_general | solution.py:57
  337.6 1.4 fusion.17
  340.3 4.4 fusion
  344.6 3.2 copy.31
  347.9 10.3 %all-to-all-start.2 = ((bf16[64,2,128,128]{3,2,1,0:T(8,128)(2,1)}), bf16[64,2,128,128]{3,2,1,0:T(8,128)(2,1)}, u32[]{:S(2)}, u32[]{:S(2)}) async-start(bf16[64,2,128,128]{3,2,1,0:T(8,128)(2,1)} %bitcast.61), calls=%async_computation.2 | async-start | bytes 8388608 | tf_op jit(solution)/shard_map/all_to_all | solution.py:65
  358.2 94.4 %all-to-all-done.2 = bf16[64,2,128,128]{3,2,1,0:T(8,128)(2,1)} async-done(((bf16[64,2,128,128]{3,2,1,0:T(8,128)(2,1)}), bf16[64,2,128,128]{3,2,1,0:T(8,128)(2,1)}, u32[]{:S(2)}, u32[]{:S(2)}) %all-to-all-start.2) | async-done | bytes 4194336 | tf_op jit(solution)/shard_map/all_to_all | solution.py:65
  452.6 2.9 gather_fusion.4
  455.5 1.1 bitcast_select_fusion
  (37 shorter events, 1.6 us)
Async XLA Ops:
  6.5 109.4 %all-reduce.2.cloned.1.call-start = ((), (), s32[]{:S(2)}) async-start(), calls=%async_computation.3 | async-start | bytes 6291456 | tf_op jit(solution)/shard_map/psum | solution.py:23
  10.1 2.9 copy-start
  10.1 2.9 copy-start.5
  10.1 18.7 %copy-start.1 = (bf16[128,1536]{1,0:T(8,128)(2,1)S(1)}, bf16[128,1536]{1,0:T(8,128)(2,1)}, u32[]{:S(2)}) copy-start(bf16[128,1536]{1,0:T(8,128)(2,1)} %param.5) | copy-start | bytes 1179652
  13.9 0.5 copy-start.3
  16.7 116.0 %all-to-all-start = ((s32[1,64,2]{2,0,1:T(1,128)}), s32[1,64,2]{2,0,1:T(1,128)}, u32[]{:S(2)}, u32[]{:S(2)}) async-start(s32[1,64,2]{2,0,1:T(1,128)} %bitcast.4), calls=%async_computation | async-start | bytes 65536 | tf_op jit(solution)/shard_map/all_to_all | solution.py:41
  132.8 193.2 %all-to-all-start.1 = ((bf16[128,64,2,256]{3,0,2,1:T(8,128)(2,1)}), bf16[128,64,2,256]{3,0,2,1:T(8,128)(2,1)}, u32[]{:S(2)}, u32[]{:S(2)}) async-start(bf16[128,64,2,256]{3,0,2,1:T(8,128)(2,1)} %select_select_fusion), calls=%async_computation.1 | async-start | bytes 16777216 | tf_op jit(solution)/shard_map/all_to_all | solution.py:40
  347.9 10.3 %copy-start.4 = (s32[32]{0:T(128)S(1)}, s32[32]{0:T(128)}, u32[]{:S(2)}) copy-start(s32[32]{0:T(128)} %copy-done.3) | copy-start | bytes 388
  347.9 107.6 %copy-start.2 = (pred[32]{0:T(512)(128)(4,1)S(1)}, pred[32]{0:T(512)(128)(4,1)}, u32[]{:S(2)}) copy-start(pred[32]{0:T(512)(128)(4,1)} %get-tuple-element.7) | copy-start | bytes 100
  347.9 104.7 %all-to-all-start.2 = ((bf16[64,2,128,128]{3,2,1,0:T(8,128)(2,1)}), bf16[64,2,128,128]{3,2,1,0:T(8,128)(2,1)}, u32[]{:S(2)}, u32[]{:S(2)}) async-start(bf16[64,2,128,128]{3,2,1,0:T(8,128)(2,1)} %bitcast.61), calls=%async_computation.2 | async-start | bytes 8388608 | tf_op jit(solution)/shard_map/all_to_all | solution.py:65
Sparse Core Ops, SparseCore 0:
  13.1 102.7 all-reduce.1
where the time goes:
time: 465 us; the launch traced here: 464 us
  waiting for transfers between devices  360 us (77%)
  starting transfers between devices  32.8 us (7%)
  local copies, waits for them, and re-layouts  25.9 us (6%)
  other arithmetic  18.4 us (4%)
  between operations  15 us (3%)
  matrix products  11.5 us (2%)
    all_to_all x1, waiting for transfers between devices, shards(): lax.all_to_all(packed, 'dp', split_axis=1, concat_axis=1, tiled=True)  180 us
    all_to_all x1, waiting for transfers between devices, shards(): lax.all_to_all(normed, 'dp', split_axis=0, concat_axis=0, tiled=True)  94.4 us
    psum x1, waiting for transfers between devices, shards(): lax.psum(grad_terms[0].astype(jnp.float32).astype(jnp.bfloat16), 'tensor')  85.5 us
    all_to_all x1, starting transfers between devices, shards(): lax.all_to_all(slot_idx.reshape(1, owners, SLOTS), 'dp', split_axis=1, co...  11.8 us
    all_to_all x1, starting transfers between devices, shards(): lax.all_to_all(packed, 'dp', split_axis=1, concat_axis=1, tiled=True)  10.7 us
    all_to_all x1, starting transfers between devices, shards(): lax.all_to_all(normed, 'dp', split_axis=0, concat_axis=0, tiled=True)  10.3 us
  transfers between devices with their start and end apart: 4, of which 3 were waited for; matrix products, arithmetic and copies ran while one was open for 5% of the time, Pallas kernels for 0%

commit v1 on v0

v1 whole, which is shorter than its diff:
```python
import jax
import jax.numpy as jnp
from jax import lax
from jax.sharding import PartitionSpec as P

BLOCK = 128
POOL = 4


epsilon = 1e-06


def pool_places(kept, starts, blocks):
    owners = starts.shape[0]
    mine = kept[0]
    everyone = lax.all_gather(kept, "dp", axis=0, tiled=True).reshape(-1)
    ids = jnp.arange(blocks, dtype=jnp.int32)
    marked = jnp.any(everyone[:, None] == ids[None, :], axis=0)
    region = jnp.sum((starts[None, :] <= mine[:, None]).astype(jnp.int32), axis=1) - 1
    first = jnp.sum(
        jnp.where(region[:, None] == jnp.arange(owners)[None, :], starts[None, :], 0), axis=1
    )
    before = marked[None, :] & (ids[None, :] >= first[:, None]) & (ids[None, :] < mine[:, None])
    place = region * POOL + jnp.sum(before.astype(jnp.int32), axis=1)
    ends = jnp.concatenate([starts[1:], jnp.full((1,), blocks, jnp.int32)])
    inside = marked[None, :] & (ids[None, :] >= starts[:, None]) & (ids[None, :] < ends[:, None])
    count = jnp.sum(inside.astype(jnp.float32), axis=1)
    return place, count


def shards(grad_terms, acts, kept, starts):
    tok_rows = acts.shape[0]
    features = grad_terms.shape[2]
    col_blocks = features // BLOCK
    row_blocks = acts.shape[1] // BLOCK
    owners = lax.axis_size("dp")
    places = owners * POOL
    chosen = kept[0, 0]
    slots = chosen.shape[0]
    place, count = pool_places(kept[0], starts[0], row_blocks * col_blocks)
    summed = lax.psum(grad_terms[0], "tensor")
    sel_a = jnp.take(acts.reshape(tok_rows, row_blocks, BLOCK), chosen // col_blocks, axis=1)
    sel_g = jnp.take(summed.reshape(tok_rows, col_blocks, BLOCK), chosen % col_blocks, axis=1)
    tiles = jnp.einsum("tkr,tkc->krc", sel_a, sel_g, preferred_element_type=jnp.float32)
    tiles = tiles.astype(jnp.bfloat16)
    hit = place[None, :] == jnp.arange(places, dtype=jnp.int32)[:, None]
    source = jnp.sum(jnp.where(hit, jnp.arange(slots, dtype=jnp.int32)[None, :], 0), axis=1)
    filled = jnp.any(hit, axis=1)
    terms = jnp.where(filled[:, None, None], jnp.take(tiles, source, axis=0), jnp.zeros((), jnp.bfloat16))
    totals = lax.psum_scatter(terms, "dp", scatter_dimension=0, tiled=True).astype(jnp.float32)
    me = lax.axis_index("dp")
    energy = jnp.sum(totals * totals)
    mean_sq = energy / (lax.dynamic_index_in_dim(count, me, keepdims=False) * (BLOCK * BLOCK))
    normed = (totals * lax.rsqrt(mean_sq + epsilon)).astype(jnp.bfloat16)
    gathered = lax.all_gather(normed, "dp", axis=0, tiled=True)
    return jnp.take(gathered, place, axis=0)[None, None]


def solution(mesh):
    placed = (
        P("tensor", "dp", None),
        P("dp", "tensor"),
        P("dp", "tensor", None),
        P("tensor", None),
    )
    return jax.shard_map(
        shards,
        mesh=mesh,
        in_specs=placed,
        out_specs=P("dp", "tensor", None, None, None),
        check_vma=False,
    )
```

time: 465 us -> 396 us (0.85)
  waiting for transfers between devices: 360 us -> 302 us
  blocking collectives: 0 us -> 39.7 us
  starting transfers between devices: 32.8 us -> 0.09 us
  matrix products: 11.5 us -> 0.6 us
    all_to_all x3 -> x0, waiting for transfers between devices: 274 us -> none  [the longest x1 180 us: shards(): lax.all_to_all(packed, 'dp', split_axis=1, concat_axis=1, tiled=True)]
    reduce_scatter x0 -> x1, waiting for transfers between devices: none -> 151 us  [shards(): lax.psum_scatter(terms, 'dp', scatter_dimension=0, tiled=True)]
    all_gather x0 -> x1, waiting for transfers between devices: none -> 92.1 us  [shards(): gathered = lax.all_gather(normed, 'dp', axis=0, tiled=True)]
    all_gather x0 -> x1, blocking collectives: none -> 39.7 us  [pool_places(): everyone = lax.all_gather(kept, 'dp', axis=0, tiled=True).reshape(-1)]
    all_to_all x3 -> x0, starting transfers between devices: 32.8 us -> none  [the longest x1 11.8 us: shards(): lax.all_to_all(slot_idx.reshape(1, owners, SLOTS), 'dp', split_axis=1, co...]
    psum x1, waiting for transfers between devices: 85.5 us -> 58.4 us  [shards(): summed = lax.psum(grad_terms[0], 'tensor')]
    dot_general x2 -> x1, matrix products: 11.5 us -> 0.6 us  [shards(): jnp.einsum('tkr,tkc->krc', sel_a, sel_g, preferred_element_type=jnp.float32)]
    gather x6 -> x4, local copies, waits for them, and re-layouts: 14 us -> 15.8 us  [the longest x1 8.3 us: shards(): jnp.take(tiles, source, axis=0)]
  transfers between devices with their start and end apart: 4 -> 3, of which waited for: 3 -> 3; matrix products, arithmetic and copies ran while one was open for 5% -> 1% of each run, Pallas kernels for 0% -> 0%
where the time goes in v1:
time: 396 us
  waiting for transfers between devices  302 us (76%)
  blocking collectives  39.7 us (10%)
  local copies, waits for them, and re-layouts  23.9 us (6%)
  other arithmetic  15.2 us (4%)
  between operations  14.6 us (4%)
    reduce_scatter x1, waiting for transfers between devices, shards(): lax.psum_scatter(terms, 'dp', scatter_dimension=0, tiled=True)  151 us
    all_gather x1, waiting for transfers between devices, shards(): gathered = lax.all_gather(normed, 'dp', axis=0, tiled=True)  92.1 us
    psum x1, waiting for transfers between devices, shards(): summed = lax.psum(grad_terms[0], 'tensor')  58.4 us
    all_gather x1, blocking collectives, pool_places(): everyone = lax.all_gather(kept, 'dp', axis=0, tiled=True).reshape(-1)  39.7 us
    gather x1, local copies, waits for them, and re-layouts, shards(): jnp.take(tiles, source, axis=0)  8.3 us
  transfers between devices with their start and end apart: 3, of which 3 were waited for; matrix products, arithmetic and copies ran while one was open for 1% of the time, Pallas kernels for 0%

profile of v1, /device:TPU:1, one launch (start us, length us, event | category | flops | bytes accessed | tf_op | source)
XLA Modules:
  0.0 395.9 jit_solution(10807428373953808137)
XLA Ops:
  6.5 3.5 copy.21
  10.1 2.8 copy.22
  12.9 0.0 reduce-scatter.2.cloned.1.call-start
  13.0 39.7 %all-gather = s32[64,1,32]{2,1,0:T(1,128)S(1)} all-gather(s32[1,1,32]{2,1,0:T(1,128)S(1)} %copy-done.1), channel_id=2, replica_groups=mesh['dp'=64,'tensor'=8] {'dp'}, dimensions={0}, use_global_device_ids=true | all-gather | bytes 8320 | tf_op jit(solution)/shard_map/all_gather | solution.py:16
  52.7 0.5 broadcast.280
  53.2 0.7 reduce.3
  53.9 0.1 eq.22
  54.0 0.2 copy.19
  54.2 0.2 copy.20
  54.5 0.7 gather_fusion
  55.3 0.2 convert_reduce_fusion.2
  55.5 0.2 select_reduce_fusion.1
  55.7 1.4 fusion
  57.1 0.2 convert_reduce_fusion.1
  57.3 0.1 select_reduce_fusion
  57.4 0.1 fusion.14
  57.5 58.4 %all-reduce.2.cloned.1.call-done = bf16[128,96,128]{2,0,1:T(8,128)(2,1)} async-done(((bf16[128,96,128]{2,0,1:T(8,128)(2,1)}), bf16[128,96,128]{2,0,1:T(8,128)(2,1)}) %all-reduce.2.cloned.1.call-update) | async-done | bytes 3145744 | tf_op jit(solution)/shard_map/psum | solution.py:41
  115.9 2.6 gather_fusion.1
  118.5 0.6 convolution_convert_fusion
  119.1 8.3 %gather_fusion.2 = bf16[256,128,128]{2,1,0:T(8,128)(2,1)} fusion(bf16[32,128,128]{2,1,0:T(8,128)(2,1)S(1)} %convolution_convert_fusion, s32[1024]{0:T(1024)S(1)} %pad_clamp_fusion.1), kind=kCustom, calls=%fused_computation.2 | custom fusion | bytes 16778240 | tf_op jit(solution)/shard_map/jit(_take)/gather | solution.py:49
  127.4 7.7 %select_select_fusion = bf16[256,128,128]{2,1,0:T(8,128)(2,1)} fusion(bf16[256,128,128]{2,1,0:T(8,128)(2,1)} %gather_fusion.2, pred[256]{0:T(512)(128)(4,1)S(1)} %compare_and_fusion.2, pred[256]{0:T(512)(128)(4,1)S(1)} %fusion.14), kind=kLoop, calls=%fused_computation.6 | loop fusion | flops 8388608 | bytes 16777728 | tf_op jit(solution)/shard_map/jit(_where)/select_n | solution.py:49
  135.1 0.0 all-gather.3.cloned.1.call-start
  135.2 0.1 slice_bitcast_fusion
  135.2 0.1 pad_add_fusion
  135.3 0.2 convert_reduce_fusion
  135.6 0.6 dynamic_slice.4
  136.8 151.2 %reduce-scatter.2.cloned.1.call-done = bf16[4,128,128]{2,1,0:T(8,128)(2,1)} async-done(((bf16[256,128,128]{2,1,0:T(8,128)(2,1)}), bf16[4,128,128]{2,1,0:T(8,128)(2,1)}) %reduce-scatter.2.cloned.1.call-update) | async-done | bytes 131088 | tf_op jit(solution)/shard_map/reduce_scatter | solution.py:50
  288.1 1.6 fusion.10
  290.3 1.6 fusion.11
  292.0 92.1 %all-gather.3.cloned.1.call-done = bf16[256,128,128]{2,1,0:T(8,128)(2,1)} async-done(((bf16[4,128,128]{2,1,0:T(8,128)(2,1)}), bf16[256,128,128]{2,1,0:T(8,128)(2,1)}) %all-gather.3.cloned.1.call-update) | async-done | bytes 8388624 | tf_op jit(solution)/shard_map/all_gather | solution.py:55
  384.1 4.1 %gather_fusion.3 = bf16[32,128,128]{2,1,0:T(8,128)(2,1)S(1)} fusion(bf16[256,128,128]{2,1,0:T(8,128)(2,1)} %all-gather.3.cloned.1.call-done, s32[1024]{0:T(1024)S(1)} %pad_clamp_fusion), kind=kCustom, calls=%fused_computation.3 | custom fusion | bytes 2097280 | tf_op jit(solution)/shard_map/jit(_take)/gather | solution.py:56
  388.2 1.1 bitcast_select_fusion
  (20 shorter events, 0.2 us)
Async XLA Ops:
  6.5 6.5 %copy-start.1 = (s32[1,1,32]{2,1,0:T(1,128)S(1)}, s32[1,1,32]{2,1,0:T(1,128)}, u32[]{:S(2)}) copy-start(s32[1,1,32]{2,1,0:T(1,128)} %param.6) | copy-start | bytes 388
  6.5 47.5 %copy-start = (bf16[128,1536]{1,0:T(8,128)(2,1)S(1)}, bf16[128,1536]{1,0:T(8,128)(2,1)}, u32[]{:S(2)}) copy-start(bf16[128,1536]{1,0:T(8,128)(2,1)} %param.5) | copy-start | bytes 1179652
  6.5 48.7 %copy-start.2 = (s32[1,64]{1,0:T(1,128)S(1)}, s32[1,64]{1,0:T(1,128)}, u32[]{:S(2)}) copy-start(s32[1,64]{1,0:T(1,128)} %param.7) | copy-start | bytes 772
  6.5 109.3 %all-reduce.2.cloned.1.call-start = ((), (), s32[]{:S(2)}) async-start(), calls=%async_computation.1 | async-start | bytes 6291456 | tf_op jit(solution)/shard_map/psum | solution.py:41
  12.9 275.1 %reduce-scatter.2.cloned.1.call-start = ((), (), s32[]{:S(2)}) async-start(), calls=%async_computation.2 | async-start | bytes 8519680 | tf_op jit(solution)/shard_map/reduce_scatter | solution.py:50
  135.1 249.0 %all-gather.3.cloned.1.call-start = ((), (), s32[]{:S(2)}) async-start(), calls=%async_computation.3 | async-start | bytes 8519680 | tf_op jit(solution)/shard_map/all_gather | solution.py:55
Sparse Core Ops, SparseCore 0:
  13.1 102.7 all-reduce.1
  135.2 152.7 reduce-scatter.1
  292.1 91.9 all-gather.2

commit v2 on v1

v2 whole, which is shorter than its diff:
```python
import functools

import jax
import jax.numpy as jnp
from jax import lax
from jax.experimental import pallas as pl
from jax.experimental.pallas import tpu as pltpu
from jax.sharding import PartitionSpec as P

BLOCK = 128
POOL = 4
ROW = 8
SUBS = 4
BATCHES = 4

epsilon = 1e-06
MESH = pl.DeviceIdType.MESH
f32, bf16, i32 = jnp.float32, jnp.bfloat16, jnp.int32


def body(
    Y, R, Z, NB,
    grad, acts, kept, starts, out,
    own, zr, gsum, pack, gsel, acts_t, tiles, xr, ys, yr, tot, eb, fac, full, opack,
    mine, kz, kr, marks, tab, srcv,
    kz_s, kr_s, c_s, p_s, src_s,
    own_sem, kz_sem, kr_sem, mk_sem, loc_sem, zrs_sem, za_sem, xa_sem, yrs_sem, e_sem, yag_sem, ret_sem,
):
    dp, t = lax.axis_index("dp"), lax.axis_index("tensor")
    y, s = dp // R, lax.rem(dp, R)
    K = out.shape[0]
    D = own.shape[1]
    rz, rr = BLOCK // Z, BLOCK // R
    cols = D // BLOCK
    SL = POOL * R
    KB = K // BATCHES
    owners = Y * R
    pending = []

    def z_dev(d):
        return (dp, lax.rem(t + d + Z, Z))

    def row_dev(d):
        return (y * R + lax.rem(s + d + R, R), t)

    def y_dev(d):
        return (lax.rem(y + d + Y, Y) * R + s, t)

    def send(src, dst, sems, index, device):
        copy = pltpu.make_async_remote_copy(
            src_ref=src, dst_ref=dst,
            send_sem=sems.at[(0,) + index], recv_sem=sems.at[(1,) + index],
            device_id=device, device_id_type=MESH,
        )
        copy.start()
        pending.append(copy)

    def arrived(dst, sems, index, device):
        pltpu.make_async_remote_copy(
            src_ref=dst, dst_ref=dst,
            send_sem=sems.at[(0,) + index], recv_sem=sems.at[(1,) + index],
            device_id=device, device_id_type=MESH,
        ).wait_recv()

    barrier = pltpu.get_barrier_semaphore()
    partners = [z_dev(d) for d in range(1, Z)] + [row_dev(d) for d in range(1, R)]
    partners += [y_dev(1)] + ([y_dev(-1)] if Y > 2 else [])
    for device in partners:
        pl.semaphore_signal(barrier, inc=1, device_id=device, device_id_type=MESH)
    mine[...] = jnp.full(mine.shape, -1, i32)
    mine[0:1, 0:K] = kept[...]
    for i in range(Z):
        rows = pl.ds(pl.multiple_of(i * rz, rz), rz)
        pltpu.make_async_copy(grad.at[0, rows, :], own.at[rows, :], own_sem.at[i]).start()
    pl.semaphore_wait(barrier, len(partners))

    for d in range(1, Z):
        send(mine, kz.at[d], kz_sem, (d,), z_dev(d))
    for d in range(1, R):
        send(mine, kr.at[d], kr_sem, (d,), row_dev(d))

    hz = Z // 2
    W = D // SUBS
    half = SUBS // 2

    def z_rows(d):
        return pl.ds(pl.multiple_of(lax.rem(t + d + Z, Z) * rz, rz), rz)

    def z_cols(q):
        return pl.ds(q * W, W)

    def z_send(w, j, q, src):
        send(src, zr.at[w, j, :, z_cols(q)], zrs_sem, (w, j, q), z_dev(1 - 2 * w))

    def z_arrived(w, j, q):
        arrived(zr.at[w, j, :, z_cols(q)], zrs_sem, (w, j, q), z_dev(1 - 2 * w))

    firsts = (range(half), range(half, SUBS))
    for i in range(half):
        for w in range(2):
            q = firsts[w][i]
            z_send(w, 0, q, grad.at[0, z_rows((1 - 2 * w) * hz), z_cols(q)])
    if hz > 1:
        for i in range(half):
            for w in range(2):
                q = firsts[1 - w][i]
                z_send(w, 1, q, grad.at[0, z_rows((1 - 2 * w) * (hz - 1)), z_cols(q)])

    for i in range(acts.shape[1] // BLOCK):
        block = acts[:, i * BLOCK:(i + 1) * BLOCK].astype(f32)
        acts_t[i] = block.T.astype(bf16)
    xr[:, K] = jnp.zeros((R, rr, BLOCK), bf16)
    for i in range(Z):
        rows = pl.ds(pl.multiple_of(i * rz, rz), rz)
        pltpu.make_async_copy(grad.at[0, rows, :], own.at[rows, :], own_sem.at[i]).wait()

    ids = lax.broadcasted_iota(i32, tab.shape, 0) * BLOCK + lax.broadcasted_iota(i32, tab.shape, 1)

    def to_smem(src, dst, i):
        copy = pltpu.make_async_copy(src, dst, loc_sem.at[i])
        copy.start()
        copy.wait()

    def marks_first():
        kz[0] = mine[...]
        kr[0] = mine[...]
        for d in range(1, Z):
            arrived(kz.at[d], kz_sem, (d,), z_dev(-d))
        for d in range(1, R):
            arrived(kr.at[d], kr_sem, (d,), row_dev(-d))
        to_smem(kz, kz_s, 0)
        to_smem(kr, kr_s, 1)

        def mark(k, m):
            for d in range(R):
                m = jnp.where(ids == kr_s[d, 0, k], 1, m)
            return m

        marks[y] = lax.fori_loop(0, K, mark, jnp.zeros(tab.shape, i32))

    hy = Y // 2

    def marks_step(j):
        if j > 0:
            for w in range(2):
                if w == 0 or j < hy:
                    place = lax.rem(y - (1 - 2 * w) * j + Y, Y)
                    arrived(marks.at[place], mk_sem, (w, j - 1), y_dev(1 - 2 * w))
        for w in range(2):
            if j < hy and (w == 0 or j < hy - 1):
                place = lax.rem(y - (1 - 2 * w) * j + Y, Y)
                send(marks.at[place], marks.at[place], mk_sem, (w, j), y_dev(1 - 2 * w))

    def places():
        m = marks[0]
        for i in range(1, Y):
            m = jnp.maximum(m, marks[i])
        lane = lax.broadcasted_iota(i32, tab.shape, 1)
        sub = lax.broadcasted_iota(i32, tab.shape, 0)
        run = m
        step = 1
        while step < BLOCK:
            run = run + jnp.where(lane >= step, pltpu.roll(run, step, 1), 0)
            step *= 2
        total = jnp.broadcast_to(run[:, BLOCK - 1:BLOCK], tab.shape)
        above = total
        step = 1
        while step < tab.shape[0]:
            above = above + jnp.where(sub >= step, pltpu.roll(above, step, 0), 0)
            step *= 2
        count = run + above - total - m
        tab[...] = count
        to_smem(tab, c_s, 2)

        def region(o, carry):
            base, before = carry
            first = starts[0, o]
            inside = ids >= first
            there = c_s[first >> 7, first & 127]
            return jnp.where(inside, o * POOL, base), jnp.where(inside, there, before)

        zero = jnp.zeros(tab.shape, i32)
        base, before = lax.fori_loop(0, owners, region, (zero, zero))
        tab[...] = base + count - before
        to_smem(tab, p_s, 3)

    def place_of(d, k):
        block = kr_s[d, 0, k]
        return p_s[block >> 7, block & 127]

    def sources():
        at = lax.broadcasted_iota(i32, (8, BLOCK), 0) * BLOCK + lax.broadcasted_iota(i32, (8, BLOCK), 1)
        for d in range(R):
            def fill(k, row):
                return jnp.where(at == place_of(d, k), k, row)

            srcv[d] = lax.fori_loop(0, K, fill, jnp.full((8, BLOCK), K, i32))
        to_smem(srcv, src_s, 4)

    order = (tuple(firsts[1]) + tuple(firsts[0]), tuple(firsts[0]) + tuple(firsts[1]))
    CH = min(512, W)

    def z_add(w, j, q, d):
        rows = z_rows(d)

        def add(c, _):
            at = pl.ds(pl.multiple_of(q * W + c * CH, CH), CH)
            zr[w, j, :, at] = (zr[w, j, :, at].astype(f32) + own[rows, at].astype(f32)).astype(bf16)
            return 0

        lax.fori_loop(0, W // CH, add, 0)

    marks_first()
    marks_step(0)
    for j in range(1, hz):
        for i in range(SUBS):
            for w in range(2):
                q = order[w][i]
                if j == 1 and q not in firsts[w]:
                    continue
                z_arrived(w, j - 1, q)
                z_add(w, j - 1, q, (1 - 2 * w) * (hz - j))
                z_send(w, j, q, zr.at[w, j - 1, :, z_cols(q)])
        if j <= hy:
            marks_step(j)
    for j in range(max(hz, 1), hy + 1):
        marks_step(j)
    places()
    sources()
    mine_rows = z_rows(0)
    for q in range(SUBS):
        for w in range(2):
            if hz > 1 or q in firsts[w]:
                z_arrived(w, hz - 1, q)

        def total_cols(c, _):
            at = pl.ds(pl.multiple_of(q * W + c * CH, CH), CH)
            sum_ = own[mine_rows, at].astype(f32)
            for w in range(2):
                if hz > 1 or q in firsts[w]:
                    sum_ = sum_ + zr[w, hz - 1, :, at].astype(f32)
            for i in range(CH // BLOCK):
                gsum[q * (W // BLOCK) + c * (CH // BLOCK) + i] = sum_[:, i * BLOCK:(i + 1) * BLOCK].astype(bf16)
            return 0

        lax.fori_loop(0, W // CH, total_cols, 0)

    far = sorted(range(1, Z), key=lambda d: -min(d, Z - d))
    for b in range(BATCHES):
        batch = pl.ds(b * KB, KB)
        for d in far:
            def put(i, _):
                col = lax.rem(kz_s[(Z - d) % Z, 0, b * KB + i], cols)
                pack[d, b * KB + i] = gsum[col]
                return 0

            lax.fori_loop(0, KB, put, 0)
            send(pack.at[d, batch], gsel.at[t, batch], za_sem, (d, b), z_dev(d))

        def keep(i, _):
            col = lax.rem(kz_s[0, 0, b * KB + i], cols)
            gsel[t, b * KB + i] = gsum[col]
            return 0

        lax.fori_loop(0, KB, keep, 0)

    for b in range(BATCHES):
        batch = pl.ds(b * KB, KB)
        for d in far:
            arrived(gsel.at[lax.rem(t - d + Z, Z), batch], za_sem, (d, b), z_dev(-d))

        def tile(i, _):
            k = b * KB + i
            left = acts_t[lax.div(kr_s[0, 0, k], cols)]
            right = gsel[:, k].reshape(BLOCK, BLOCK)
            product = jnp.dot(left, right, preferred_element_type=f32).astype(bf16)
            tiles[:, k] = product.reshape(R, rr, BLOCK)
            xr[0, k] = tiles[s, k]
            return 0

        lax.fori_loop(0, KB, tile, 0)
        for d in range(1, R):
            send(tiles.at[lax.rem(s + d, R), batch], xr.at[d, batch], xa_sem, (d, b), row_dev(d))
    for b in range(BATCHES):
        for d in range(1, R):
            arrived(xr.at[d, pl.ds(b * KB, KB)], xa_sem, (d, b), row_dev(-d))

    HS = SL // 2

    def y_at(d, p):
        return lax.rem(y + d + Y, Y) * SL + p

    def slot_sum(place):
        sum_ = jnp.zeros((rr, BLOCK), f32)
        for d in range(R):
            sum_ = sum_ + xr[d, src_s[d, place >> 7, place & 127]].astype(f32)
        return sum_

    def y_send(w, j, h, src):
        send(src, yr.at[w, j, pl.ds(h * HS, HS)], yrs_sem, (w, j, h), y_dev(1 - 2 * w))

    def y_arrived(w, j, h):
        arrived(yr.at[w, j, pl.ds(h * HS, HS)], yrs_sem, (w, j, h), y_dev(1 - 2 * w))

    def y_first(w, j, h):
        def one(p, _):
            ys[w, j, p] = slot_sum(y_at((1 - 2 * w) * (hy - j), h * HS + p)).astype(bf16)
            return 0

        lax.fori_loop(0, HS, one, 0)
        y_send(w, j, h, ys.at[w, j])

    for w in range(2):
        y_first(w, 0, w)
    if hy > 1:
        for w in range(2):
            y_first(w, 1, 1 - w)
    for j in range(1, hy):
        for i in range(2):
            for w in range(2):
                h = (1 - w, w)[i]
                if j == 1 and h != w:
                    continue
                y_arrived(w, j - 1, h)

                def one(p, _):
                    slot = h * HS + p
                    there = slot_sum(y_at((1 - 2 * w) * (hy - j), slot))
                    yr[w, j - 1, slot] = (yr[w, j - 1, slot].astype(f32) + there).astype(bf16)
                    return 0

                lax.fori_loop(0, HS, one, 0)
                y_send(w, j, h, yr.at[w, j - 1, pl.ds(h * HS, HS)])
    def own_sum(p, _):
        tot[p] = slot_sum(y_at(0, p))
        return 0

    lax.fori_loop(0, SL, own_sum, 0)
    for h in range(2):
        for w in range(2):
            if hy > 1 or h == w:
                y_arrived(w, hy - 1, h)
    sub8 = lax.broadcasted_iota(i32, (8, BLOCK), 0)
    energy = jnp.zeros((8, BLOCK), f32)
    for h in range(2):
        def squares(g, energy):
            here = jnp.zeros((rr, BLOCK), f32)
            for i in range(POOL):
                p = g * POOL + i
                value = tot[p]
                for w in range(2):
                    if hy > 1 or h == w:
                        value = value + yr[w, hy - 1, p].astype(f32)
                tot[p] = value
                here = here + value * value
            line = jnp.sum(here, axis=0, keepdims=True)
            return jnp.where(sub8 == g, line, energy)

        energy = lax.fori_loop(h * (R // 2), (h + 1) * (R // 2), squares, energy)
    eb[0] = energy
    for d in range(1, R):
        send(eb.at[0], eb.at[d], e_sem, (d,), row_dev(d))
    count = jnp.zeros((8, BLOCK), i32)
    for g in range(R):
        o = y * R + g
        first = starts[0, o]
        after = starts[0, jnp.minimum(o + 1, owners - 1)]
        after = jnp.where(o + 1 < owners, after, NB)
        n = c_s[after >> 7, after & 127] - c_s[first >> 7, first & 127]
        count = jnp.where(sub8 == g, n, count)
    for d in range(1, R):
        arrived(eb.at[d], e_sem, (d,), row_dev(-d))
        energy = energy + eb[d]
    count = jnp.maximum(count, 1).astype(f32)
    mean_sq = jnp.sum(energy, axis=1, keepdims=True) / (count * (BLOCK * BLOCK))
    fac[...] = lax.rsqrt(mean_sq + epsilon)

    def scale(p, _):
        full[y * SL + p] = (tot[p] * fac[pl.ds(p >> 2, 1), :]).astype(bf16)
        return 0

    def ag_part(w, j, h):
        return full.at[pl.ds(y_at(-(1 - 2 * w) * j, h * HS), HS)]

    def ag_send(w, j, h):
        send(ag_part(w, j, h), ag_part(w, j, h), yag_sem, (w, j, h), y_dev(1 - 2 * w))

    for h in range(2):
        lax.fori_loop(h * HS, (h + 1) * HS, scale, 0)
        for w in range(2):
            if hy > 1 or h == w:
                ag_send(w, 0, h)
    for j in range(1, hy + 1):
        for h in range(2):
            for w in range(2):
                if j == hy and h != w:
                    continue
                arrived(ag_part(w, j, h), yag_sem, (w, j - 1, h), y_dev(1 - 2 * w))
                if j < hy - 1 or (j == hy - 1 and h == w):
                    ag_send(w, j, h)

    slice_ = pl.ds(pl.multiple_of(s * rr, rr), rr)
    near = sorted(range(1, R), key=lambda d: -min(d, R - d))
    for b in range(BATCHES):
        batch = pl.ds(b * KB, KB)
        for d in near:
            def put(i, _):
                k = b * KB + i
                opack[d, k] = full[place_of((R - d) % R, k)]
                return 0

            lax.fori_loop(0, KB, put, 0)
            send(opack.at[d, batch], out.at[batch, slice_, :], ret_sem, (d, b), row_dev(d))

    def keep_own(k, _):
        out[k, slice_, :] = full[place_of(0, k)]
        return 0

    lax.fori_loop(0, K, keep_own, 0)
    for b in range(BATCHES):
        for d in near:
            rows = pl.ds(pl.multiple_of(lax.rem(s - d + R, R) * rr, rr), rr)
            arrived(out.at[pl.ds(b * KB, KB), rows, :], ret_sem, (d, b), row_dev(-d))
    for copy in pending:
        copy.wait_send()


def shards(R, Z, grad_terms, acts, kept, starts):
    Y = lax.axis_size("dp") // R
    tokens, D = grad_terms.shape[1:]
    K = kept.shape[2]
    NB = (acts.shape[1] // BLOCK) * (D // BLOCK)
    rz, rr = BLOCK // Z, BLOCK // R
    SL = POOL * R
    hz, hy = Z // 2, Y // 2
    tab = (-(-(NB // BLOCK + 1) // 8) * 8, BLOCK)
    vmem, smem, dma = pltpu.VMEM, pltpu.SMEM, pltpu.SemaphoreType.DMA
    in_vmem = pl.BlockSpec(memory_space=pltpu.VMEM)
    result = pl.pallas_call(
        functools.partial(body, Y, R, Z, NB),
        out_shape=jax.ShapeDtypeStruct((K, BLOCK, BLOCK), bf16),
        in_specs=[
            pl.BlockSpec(memory_space=pl.ANY),
            in_vmem,
            in_vmem,
            pl.BlockSpec(memory_space=pltpu.SMEM),
        ],
        out_specs=in_vmem,
        scratch_shapes=[
            vmem((tokens, D), bf16),
            vmem((2, hz, rz, D), bf16),
            vmem((D // BLOCK, rz, BLOCK), bf16),
            vmem((Z, K, rz, BLOCK), bf16),
            vmem((Z, K, rz, BLOCK), bf16),
            vmem((acts.shape[1] // BLOCK, BLOCK, BLOCK), bf16),
            vmem((R, K, rr, BLOCK), bf16),
            vmem((R, K + 1, rr, BLOCK), bf16),
            vmem((2, 2, SL // 2, rr, BLOCK), bf16),
            vmem((2, hy, SL, rr, BLOCK), bf16),
            vmem((SL, rr, BLOCK), f32),
            vmem((R, 8, BLOCK), f32),
            vmem((8, BLOCK), f32),
            vmem((Y * SL, rr, BLOCK), bf16),
            vmem((R, K, rr, BLOCK), bf16),
            vmem((8, BLOCK), i32),
            vmem((Z, 8, BLOCK), i32),
            vmem((R, 8, BLOCK), i32),
            vmem((Y,) + tab, i32),
            vmem(tab, i32),
            vmem((R, 8, BLOCK), i32),
            smem((Z, 8, BLOCK), i32),
            smem((R, 8, BLOCK), i32),
            smem(tab, i32),
            smem(tab, i32),
            smem((R, 8, BLOCK), i32),
            dma((Z,)),
            dma((2, Z)),
            dma((2, R)),
            dma((2, 2, hy)),
            dma((5,)),
            dma((2, 2, hz, SUBS)),
            dma((2, Z, BATCHES)),
            dma((2, R, BATCHES)),
            dma((2, 2, hy, 2)),
            dma((2, R)),
            dma((2, 2, hy, 2)),
            dma((2, R, BATCHES)),
        ],
        compiler_params=pltpu.CompilerParams(
            collective_id=0, has_side_effects=True, vmem_limit_bytes=40 * 1024 * 1024
        ),
    )(grad_terms, acts, kept[0], starts)
    return result[None, None]


def solution(mesh, row=ROW):
    placed = (
        P("tensor", "dp", None),
        P("dp", "tensor"),
        P("dp", "tensor", None),
        P("tensor", None),
    )
    return jax.shard_map(
        functools.partial(shards, row, mesh.shape["tensor"]),
        mesh=mesh,
        in_specs=placed,
        out_specs=P("dp", "tensor", None, None, None),
        check_vma=False,
    )
```

time: 396 us -> 137 us (0.35)
  waiting for transfers between devices: 302 us -> 0 us
  Pallas kernels: 0 us -> 132 us
  blocking collectives: 39.7 us -> 0 us
  local copies, waits for them, and re-layouts: 23.9 us -> 5.17 us
  other arithmetic: 15.2 us -> 0 us
  between operations: 14.6 us -> 0.01 us
    reduce_scatter x1 -> x0, waiting for transfers between devices: 151 us -> none  [shards(): lax.psum_scatter(terms, 'dp', scatter_dimension=0, tiled=True)]
    pallas_call x0 -> x1, Pallas kernels: none -> 132 us  [shards(): pl.pallas_call(functools.partial(body, Y, R, Z, NB), out_shape=jax.ShapeD...]
    all_gather x1 -> x0, waiting for transfers between devices: 92.1 us -> none  [shards(): gathered = lax.all_gather(normed, 'dp', axis=0, tiled=True)]
    psum x1 -> x0, waiting for transfers between devices: 58.4 us -> none  [shards(): summed = lax.psum(grad_terms[0], 'tensor')]
    all_gather x1 -> x0, blocking collectives: 39.7 us -> none  [pool_places(): everyone = lax.all_gather(kept, 'dp', axis=0, tiled=True).reshape(-1)]
    gather x4 -> x0, local copies, waits for them, and re-layouts: 15.8 us -> none  [the longest x1 8.3 us: shards(): jnp.take(tiles, source, axis=0)]
    select_n x5 -> x0, other arithmetic: 8.84 us -> none  [the longest x1 7.68 us: shards(): jnp.where(filled[:, None, None], jnp.take(tiles, source, axis=0), jnp.zer...]
  transfers between devices with their start and end apart: 3 -> 0, of which waited for: 3 -> 0; matrix products, arithmetic and copies ran while one was open for 1% -> 0% of each run, Pallas kernels for 0% -> 0%
where the time goes in v2:
time: 137 us
  Pallas kernels  132 us (96%)
  local copies, waits for them, and re-layouts  5.17 us (4%)
    pallas_call x1, Pallas kernels, shards(): pl.pallas_call(functools.partial(body, Y, R, Z, NB), out_shape=jax.ShapeD...  132 us
    unnamed x9, local copies, waits for them, and re-layouts  5.17 us

profile of v2, /device:TPU:1, one launch (start us, length us, event | category | flops | bytes accessed | tf_op | source)
XLA Modules:
  0.0 136.7 jit_solution(17754449366080724609)
XLA Ops:
  0.0 0.0 copy-start
  0.0 1.9 %copy-done = bf16[1,128,12288]{2,1,0:T(8,128)(2,1)S(1)} copy-done((bf16[1,128,12288]{2,1,0:T(8,128)(2,1)S(1)}, bf16[1,128,12288]{2,1,0:T(8,128)(2,1)}, u32[]{:S(2)}) %copy-start) | copy-done | bytes 3145752
  1.9 0.0 copy-start.1
  1.9 1.0 copy-done.1
  2.9 0.0 copy-start.2
  2.9 0.7 copy-done.2
  3.5 0.0 copy-start.3
  3.5 0.7 copy-done.3
  4.2 131.5 %shard_map.46 = bf16[32,128,128]{2,1,0:T(8,128)(2,1)S(1)} custom-call(bf16[1,128,12288]{2,1,0:T(8,128)(2,1)S(1)} %copy-done, bf16[128,1536]{1,0:T(8,128)(2,1)S(1)} %copy-done.1, s32[1,32]{1,0:T(1,128)S(1)} %bitcast.3, s32[1,64]{1,0:T(1,128)S(1)} %copy-done.3), custom_call_target="tpu_custom_call" | custom-call | tf_op jit(solution)/shard_map/pallas_call | solution.py:439
  135.8 1.0 copy.6
Async XLA Ops:
  0.0 1.9 %copy-start = (bf16[1,128,12288]{2,1,0:T(8,128)(2,1)S(1)}, bf16[1,128,12288]{2,1,0:T(8,128)(2,1)}, u32[]{:S(2)}) copy-start(bf16[1,128,12288]{2,1,0:T(8,128)(2,1)} %grad.1) | copy-start | bytes 9437188
  1.9 1.0 copy-start.1
  2.9 0.7 copy-start.2
  3.5 0.7 copy-start.3

commit v3 on v2

v3 whole, which is shorter than its diff:
```python
import functools

import jax
import jax.numpy as jnp
from jax import lax
from jax.experimental import pallas as pl
from jax.experimental.pallas import tpu as pltpu
from jax.sharding import PartitionSpec as P

BLOCK = 128
POOL = 4
ROW = 8
SUBS = 4
PARTS = 4
UNROLL = 8

epsilon = 1e-06
MESH = pl.DeviceIdType.MESH
f32, bf16, i32 = jnp.float32, jnp.bfloat16, jnp.int32


def body(
    Y, R, Z, NB,
    grad, acts_in, kept_in, starts_in, out,
    acts, kept, kept_s, starts, own, zr, gsum, pack, gsel, acts_t, perm, tiles, fwd, mid, xs, sel, tot,
    esq, eb, ey, fac, facs, full, back, opack, land, mine, kz, mr, my, pr, py, tab, square,
    kz_s, c_s, p_s, fac_s,
    in_sem, own_sem, kz_sem, mr_sem, my_sem, pr_sem, py_sem, loc_sem, zrs_sem, za_sem, xa_sem, ya_sem,
    er_sem, ey_sem, yag_sem, ret_sem,
):
    dp, t = lax.axis_index("dp"), lax.axis_index("tensor")
    y, s = dp // R, lax.rem(dp, R)
    K = out.shape[0]
    D = own.shape[1]
    rz, J = BLOCK // Z, BLOCK // (Y * R)
    cols = D // BLOCK
    KB = Y
    batches = K // KB
    H = KB * J
    RJ = R * J
    owners = Y * R
    SR = POOL * owners * J
    pending = []

    def z_dev(d):
        return (dp, lax.rem(t + d + Z, Z))

    def row_dev(d):
        return (y * R + lax.rem(s + d + R, R), t)

    def y_dev(d):
        return (lax.rem(y + d + Y, Y) * R + s, t)

    def send(src, dst, sems, index, device):
        copy = pltpu.make_async_remote_copy(
            src_ref=src, dst_ref=dst,
            send_sem=sems.at[(0,) + index], recv_sem=sems.at[(1,) + index],
            device_id=device, device_id_type=MESH,
        )
        copy.start()
        pending.append(copy)

    def arrived(dst, sems, index, device):
        pltpu.make_async_remote_copy(
            src_ref=dst, dst_ref=dst,
            send_sem=sems.at[(0,) + index], recv_sem=sems.at[(1,) + index],
            device_id=device, device_id_type=MESH,
        ).wait_recv()

    def loop(n, step):
        def one(i, _):
            step(i)
            return 0

        lax.fori_loop(0, n, one, 0, unroll=min(UNROLL, n))

    barrier = pltpu.get_barrier_semaphore()
    partners = [z_dev(d) for d in range(1, Z)] + [row_dev(d) for d in range(1, R)]
    partners += [y_dev(d) for d in range(1, Y)]
    for device in partners:
        pl.semaphore_signal(barrier, inc=1, device_id=device, device_id_type=MESH)
    inputs = [
        pltpu.make_async_copy(src, dst, in_sem.at[i])
        for i, (src, dst) in enumerate(((kept_in.at[0], kept), (kept_in.at[0], kept_s), (starts_in, starts), (acts_in, acts)))
    ]
    for copy in inputs:
        copy.start()
    for i in range(Z):
        rows = pl.ds(pl.multiple_of(i * rz, rz), rz)
        pltpu.make_async_copy(grad.at[0, rows, :], own.at[rows, :], own_sem.at[i]).start()
    inputs[0].wait()
    mine[...] = jnp.full(mine.shape, -1, i32)
    mine[0:1, 0:K] = kept[...]
    pl.semaphore_wait(barrier, len(partners))

    for d in range(1, Z):
        send(mine, kz.at[d], kz_sem, (d,), z_dev(d))

    hz = Z // 2
    W = D // SUBS
    half = SUBS // 2

    def z_rows(d):
        return pl.ds(pl.multiple_of(lax.rem(t + d + Z, Z) * rz, rz), rz)

    def z_cols(q):
        return pl.ds(q * W, W)

    def z_send(w, j, q, src):
        send(src, zr.at[w, j, :, z_cols(q)], zrs_sem, (w, j, q), z_dev(1 - 2 * w))

    def z_arrived(w, j, q):
        arrived(zr.at[w, j, :, z_cols(q)], zrs_sem, (w, j, q), z_dev(1 - 2 * w))

    firsts = (range(half), range(half, SUBS))
    for i in range(half):
        for w in range(2):
            q = firsts[w][i]
            z_send(w, 0, q, grad.at[0, z_rows((1 - 2 * w) * hz), z_cols(q)])
    if hz > 1:
        for i in range(half):
            for w in range(2):
                q = firsts[1 - w][i]
                z_send(w, 1, q, grad.at[0, z_rows((1 - 2 * w) * (hz - 1)), z_cols(q)])

    for copy in inputs[1:]:
        copy.wait()
    ids = lax.broadcasted_iota(i32, tab.shape, 0) * BLOCK + lax.broadcasted_iota(i32, tab.shape, 1)

    def mark(k, m):
        return jnp.where(ids == kept_s[0, k], 1, m)

    mr[0] = lax.fori_loop(0, K, mark, jnp.zeros(tab.shape, i32), unroll=min(UNROLL, K))
    for d in range(1, R):
        send(mr.at[0], mr.at[d], mr_sem, (d,), row_dev(d))
    for i in range(acts.shape[1] // BLOCK):
        block = acts[:, i * BLOCK:(i + 1) * BLOCK].astype(f32)
        acts_t[i] = block.T.astype(bf16)
    to = lax.broadcasted_iota(i32, (BLOCK, BLOCK), 0)
    frm = lax.broadcasted_iota(i32, (BLOCK, BLOCK), 1)
    for i, (outer, inner) in enumerate(((R, KB), (KB, R))):
        a, b, c = lax.div(to, inner * J), lax.rem(lax.div(to, J), inner), lax.rem(to, J)
        perm[i] = jnp.where(frm == (b * outer + a) * J + c, 1.0, 0.0).astype(bf16)
    for i in range(Z):
        rows = pl.ds(pl.multiple_of(i * rz, rz), rz)
        pltpu.make_async_copy(grad.at[0, rows, :], own.at[rows, :], own_sem.at[i]).wait()

    def to_smem(src, dst, i):
        copy = pltpu.make_async_copy(src, dst, loc_sem.at[i])
        copy.start()
        copy.wait()

    def gathered(ref, sems, dev, n):
        for d in range(1, n):
            arrived(ref.at[d], sems, (d,), dev(-d))
        m = ref[0]
        for d in range(1, n):
            m = jnp.maximum(m, ref[d])
        return m

    def marks_row():
        kz[0] = mine[...]
        for d in range(1, Z):
            arrived(kz.at[d], kz_sem, (d,), z_dev(-d))
        to_smem(kz, kz_s, 0)
        my[0] = gathered(mr, mr_sem, row_dev, R)
        for d in range(1, Y):
            send(my.at[0], my.at[d], my_sem, (d,), y_dev(d))

    def places():
        m = gathered(my, my_sem, y_dev, Y)
        lane = lax.broadcasted_iota(i32, tab.shape, 1)
        sub = lax.broadcasted_iota(i32, tab.shape, 0)
        run = m
        step = 1
        while step < BLOCK:
            run = run + jnp.where(lane >= step, pltpu.roll(run, step, 1), 0)
            step *= 2
        total = jnp.broadcast_to(run[:, BLOCK - 1:BLOCK], tab.shape)
        above = total
        step = 1
        while step < tab.shape[0]:
            above = above + jnp.where(sub >= step, pltpu.roll(above, step, 0), 0)
            step *= 2
        count = run + above - total - m
        tab[...] = count
        to_smem(tab, c_s, 1)

        def region(o, carry):
            base, before = carry
            first = starts[0, o]
            inside = ids >= first
            there = c_s[first >> 7, first & 127]
            return jnp.where(inside, o * POOL, base), jnp.where(inside, there, before)

        zero = jnp.zeros(tab.shape, i32)
        base, before = lax.fori_loop(0, owners, region, (zero, zero), unroll=UNROLL)
        tab[...] = base + count - before
        to_smem(tab, p_s, 2)

        sub8 = lax.broadcasted_iota(i32, (8, BLOCK), 0)
        lane8 = lax.broadcasted_iota(i32, (8, BLOCK), 1)

        def fill(k, tile):
            here = (sub8 == lax.div(k, KB)) & (lax.div(lane8, J) == s * KB + lax.rem(k, KB))
            return jnp.where(here, place_of(k) * J + lax.rem(lane8, J), tile)

        pr[0] = lax.fori_loop(0, K, fill, jnp.full((8, BLOCK), -1, i32), unroll=min(UNROLL, K))
        for d in range(1, R):
            send(pr.at[0], pr.at[d], pr_sem, (d,), row_dev(d))

    def place_of(k):
        block = kept_s[0, k]
        return p_s[block >> 7, block & 127]

    def places_row():
        py[y] = gathered(pr, pr_sem, row_dev, R)
        for d in range(1, Y):
            send(py.at[y], py.at[y], py_sem, (d,), y_dev(d))
        square[...] = jnp.zeros(square.shape, f32)
        square[0:8, :] = py[y].astype(f32)
        turned = square[...].T
        lane = lax.broadcasted_iota(i32, (BLOCK, SR), 1).astype(f32)
        for b in range(batches):
            back[b * BLOCK:(b + 1) * BLOCK, :] = jnp.where(turned[:, b:b + 1] == lane, 1.0, 0.0).astype(bf16)

    def places_all():
        for d in range(1, Y):
            arrived(py.at[lax.rem(y - d + Y, Y)], py_sem, (d,), y_dev(-d))

    def select(b):
        row = lax.broadcasted_iota(i32, (SR, BLOCK), 0)

        def one(i, _):
            at = pl.ds(pl.multiple_of(i * BLOCK, BLOCK), BLOCK)
            sel[b, :, at] = jnp.where(py[i][b:b + 1, :] == row, 1.0, 0.0).astype(bf16)
            return 0

        lax.fori_loop(0, Y, one, 0)

    def counts():
        lane = lax.broadcasted_iota(i32, (8, BLOCK), 1)

        def one(o, n):
            first = starts[0, o]
            after = starts[0, jnp.minimum(o + 1, owners - 1)]
            after = jnp.where(o + 1 < owners, after, NB)
            there = c_s[after >> 7, after & 127] - c_s[first >> 7, first & 127]
            return jnp.where(lane == o, there, n)

        n = lax.fori_loop(0, owners, one, jnp.ones((8, BLOCK), i32), unroll=UNROLL)
        fac[...] = jnp.maximum(n, 1).astype(f32)

    order = (tuple(firsts[1]) + tuple(firsts[0]), tuple(firsts[0]) + tuple(firsts[1]))
    CH = min(512, W)

    def z_add(w, j, q, d):
        rows = z_rows(d)

        def add(c):
            at = pl.ds(pl.multiple_of(q * W + c * CH, CH), CH)
            zr[w, j, :, at] = (zr[w, j, :, at].astype(f32) + own[rows, at].astype(f32)).astype(bf16)

        loop(W // CH, add)

    chores = [marks_row, places, places_row, places_all] + [functools.partial(select, b) for b in range(batches)] + [counts]
    for j in range(1, hz):
        for i in range(SUBS):
            for w in range(2):
                q = order[w][i]
                if j == 1 and q not in firsts[w]:
                    continue
                z_arrived(w, j - 1, q)
                z_add(w, j - 1, q, (1 - 2 * w) * (hz - j))
                z_send(w, j, q, zr.at[w, j - 1, :, z_cols(q)])
            if chores and (i % 2 or j == hz - 1) and (j > 1 or i == SUBS - 1):
                chores.pop(0)()
    for chore in chores:
        chore()
    mine_rows = z_rows(0)
    for q in range(SUBS):
        for w in range(2):
            if hz > 1 or q in firsts[w]:
                z_arrived(w, hz - 1, q)

        def total_cols(c):
            at = pl.ds(pl.multiple_of(q * W + c * CH, CH), CH)
            sum_ = own[mine_rows, at].astype(f32)
            for w in range(2):
                if hz > 1 or q in firsts[w]:
                    sum_ = sum_ + zr[w, hz - 1, :, at].astype(f32)
            for i in range(CH // BLOCK):
                gsum[q * (W // BLOCK) + c * (CH // BLOCK) + i] = sum_[:, i * BLOCK:(i + 1) * BLOCK].astype(bf16)

        loop(W // CH, total_cols)

    far = sorted(range(1, Z), key=lambda d: -min(d, Z - d))
    for b in range(batches):
        batch = pl.ds(b * KB, KB)
        for d in far:
            def put(i):
                col = lax.rem(kz_s[(Z - d) % Z, 0, b * KB + i], cols)
                pack[d, b * KB + i] = gsum[col]

            loop(KB, put)
            send(pack.at[d, batch], gsel.at[t, batch], za_sem, (d, b), z_dev(d))

        def keep(i):
            col = lax.rem(kz_s[0, 0, b * KB + i], cols)
            gsel[t, b * KB + i] = gsum[col]

        loop(KB, keep)

    for b in range(batches):
        batch = pl.ds(b * KB, KB)
        for d in far:
            arrived(gsel.at[lax.rem(t - d + Z, Z), batch], za_sem, (d, b), z_dev(-d))
        for i in range(KB):
            k = b * KB + i
            left = acts_t[lax.div(kept_s[0, k], cols)]
            right = gsel[:, k].reshape(BLOCK, BLOCK)
            product = jnp.dot(left, right, preferred_element_type=f32).astype(bf16)
            tiles[:, i] = product.reshape(Y, RJ, BLOCK)
        for i in range(Y):
            turned = jnp.dot(perm[0], tiles[i].reshape(BLOCK, BLOCK), preferred_element_type=f32)
            fwd[b, :, i] = turned.astype(bf16).reshape(R, H, BLOCK)
        for d in range(1, R):
            send(fwd.at[b, lax.rem(s + d, R)], mid.at[b, :, s], xa_sem, (d, b), row_dev(d))
        mid[b, :, s] = fwd[b, s]
        for d in range(1, R):
            arrived(mid.at[b, :, lax.rem(s - d + R, R)], xa_sem, (d, b), row_dev(-d))
        for d in sorted(range(1, Y), key=lambda d: -min(d, Y - d)):
            send(mid.at[b, lax.rem(y + d, Y)], xs.at[b, y], ya_sem, (d, b), y_dev(d))
        xs[b, y] = mid[b, y]

    for b in range(batches):
        for d in range(1, Y):
            arrived(xs.at[b, lax.rem(y - d + Y, Y)], ya_sem, (d, b), y_dev(-d))
        here = jnp.dot(sel[b], xs[b].reshape(Y * BLOCK, BLOCK), preferred_element_type=f32)
        tot[...] = here if b == 0 else tot[...] + here

    hy = Y // 2
    HS = SR // PARTS
    firsts = (range(PARTS // 2), range(PARTS // 2, PARTS))

    def y_of(d):
        return lax.rem(y + d + Y, Y)

    def ag_part(d, h):
        return full.at[y_of(d), pl.ds(h * HS, HS)]

    def ag_send(w, j, h):
        away = 1 - 2 * w
        if j < hy - 1:
            send(ag_part(-away * j, h), ag_part(-away * j, h), yag_sem, (w, j, h), y_dev(away))
        if j == hy - 2 and h in firsts[w]:
            send(ag_part(-away * j, h), ag_part(-away * j, h), yag_sem, (w, hy - 1, h), y_dev(2 * away))

    full[y] = tot[...].astype(bf16)
    for i in range(PARTS):
        for w in range(2):
            ag_send(w, 0, (i if w == 0 else PARTS - 1 - i))
    squares = jnp.sum((tot[...] * tot[...]).reshape(owners, POOL * J, BLOCK), axis=1)
    esq[...] = jnp.zeros(esq.shape, f32)
    esq[0:owners, :] = squares
    eb[0] = lax.dot_general(
        jnp.ones((8, BLOCK), f32), esq[...], (((1,), (1,)), ((), ())),
        precision=lax.Precision.HIGHEST, preferred_element_type=f32,
    )
    for d in range(1, R):
        send(eb.at[0], eb.at[d], er_sem, (d,), row_dev(d))

    near = sorted(range(1, R), key=lambda d: -min(d, R - d))

    def give(d):
        at = y_of(d)
        rows = jnp.dot(back[...], full[at], preferred_element_type=f32).astype(bf16)
        opack[at] = rows.reshape(batches, R, H, BLOCK)
        for e in near:
            send(opack.at[at, :, lax.rem(s + e, R)], land.at[at, :, s], ret_sem, (e, d % Y), row_dev(e))
        land[at, :, s] = opack[at, :, s]

    def finish(d):
        at = y_of(d)
        for e in near:
            arrived(land.at[at, :, lax.rem(s - e + R, R)], ret_sem, (e, d % Y), row_dev(-e))
        rows = pl.ds(pl.multiple_of(at * RJ, RJ), RJ)
        for b in range(batches):
            turned = jnp.dot(perm[1], land[at, b].reshape(BLOCK, BLOCK), preferred_element_type=f32)
            turned = turned.reshape(KB, RJ, BLOCK)
            for i in range(KB):
                k = b * KB + i
                out[k, rows, :] = (turned[i] * facs[k:k + 1, :]).astype(bf16)

    def energies(ref, sems, dev, n):
        sum_ = ref[0]
        for d in range(1, n):
            arrived(ref.at[d], sems, (d,), dev(-d))
            sum_ = sum_ + ref[d]
        return sum_

    def energy_row():
        ey[0] = energies(eb, er_sem, row_dev, R)
        for d in range(1, Y):
            send(ey.at[0], ey.at[d], ey_sem, (d,), y_dev(d))

    def factors():
        mean_sq = energies(ey, ey_sem, y_dev, Y) / (fac[...] * (BLOCK * BLOCK))
        fac[...] = lax.rsqrt(mean_sq + epsilon)
        to_smem(fac, fac_s, 3)

        def one(k):
            facs[pl.ds(k, 1), :] = jnp.full((1, BLOCK), fac_s[0, place_of(k) >> 2], f32)

        loop(K, one)

    give(0)
    energy_row()
    waiting = [0]
    for j in range(1, hy + 1):
        for i in range(PARTS):
            for w in range(2):
                h = i if w == 0 else PARTS - 1 - i
                if j == hy and h not in firsts[w]:
                    continue
                hop = 2 if j == hy else 1
                arrived(ag_part(-(1 - 2 * w) * j, h), yag_sem, (w, j - 1, h), y_dev(-(1 - 2 * w) * hop))
                if j < hy:
                    ag_send(w, j, h)
        come = (-j, j) if j < hy else (j,)
        for d in come:
            give(d)
        if j == 2:
            factors()
        if j > 2:
            for d in waiting[:2]:
                finish(d)
            waiting = waiting[2:]
        waiting += come
    for d in waiting:
        finish(d)
    for copy in pending:
        copy.wait_send()


def shards(R, Z, grad_terms, acts, kept, starts):
    Y = lax.axis_size("dp") // R
    tokens, D = grad_terms.shape[1:]
    K = kept.shape[2]
    NB = (acts.shape[1] // BLOCK) * (D // BLOCK)
    rz = BLOCK // Z
    hz, hy = Z // 2, Y // 2
    J = BLOCK // (Y * R)
    H = Y * J
    batches = K // Y
    SR = POOL * Y * R * J
    tab = (-(-(NB // BLOCK + 1) // 8) * 8, BLOCK)
    vmem, smem, dma = pltpu.VMEM, pltpu.SMEM, pltpu.SemaphoreType.DMA
    in_vmem = pl.BlockSpec(memory_space=pltpu.VMEM)
    result = pl.pallas_call(
        functools.partial(body, Y, R, Z, NB),
        out_shape=jax.ShapeDtypeStruct((K, BLOCK, BLOCK), bf16),
        in_specs=[pl.BlockSpec(memory_space=pltpu.HBM)] * 4,
        out_specs=in_vmem,
        scratch_shapes=[
            vmem(acts.shape, bf16),
            vmem(kept.shape[1:], i32),
            smem(kept.shape[1:], i32),
            smem(starts.shape, i32),
            vmem((tokens, D), bf16),
            vmem((2, hz, rz, D), bf16),
            vmem((D // BLOCK, rz, BLOCK), bf16),
            vmem((Z, K, rz, BLOCK), bf16),
            vmem((Z, K, rz, BLOCK), bf16),
            vmem((acts.shape[1] // BLOCK, BLOCK, BLOCK), bf16),
            vmem((2, BLOCK, BLOCK), bf16),
            vmem((Y, Y, R * J, BLOCK), bf16),
            vmem((batches, R, Y, H, BLOCK), bf16),
            vmem((batches, Y, R, H, BLOCK), bf16),
            vmem((batches, Y, R, H, BLOCK), bf16),
            vmem((batches, SR, Y * BLOCK), bf16),
            vmem((SR, BLOCK), f32),
            vmem((BLOCK, BLOCK), f32),
            vmem((R, 8, BLOCK), f32),
            vmem((Y, 8, BLOCK), f32),
            vmem((8, BLOCK), f32),
            vmem((K, BLOCK), f32),
            vmem((Y, SR, BLOCK), bf16),
            vmem((batches * BLOCK, SR), bf16),
            vmem((Y, batches, R, H, BLOCK), bf16),
            vmem((Y, batches, R, H, BLOCK), bf16),
            vmem((8, BLOCK), i32),
            vmem((Z, 8, BLOCK), i32),
            vmem((R,) + tab, i32),
            vmem((Y,) + tab, i32),
            vmem((R, 8, BLOCK), i32),
            vmem((Y, 8, BLOCK), i32),
            vmem(tab, i32),
            vmem((BLOCK, BLOCK), f32),
            smem((Z, 8, BLOCK), i32),
            smem(tab, i32),
            smem(tab, i32),
            smem((8, BLOCK), f32),
            dma((4,)),
            dma((Z,)),
            dma((2, Z)),
            dma((2, R)),
            dma((2, Y)),
            dma((2, R)),
            dma((2, Y)),
            dma((4,)),
            dma((2, 2, hz, SUBS)),
            dma((2, Z, batches)),
            dma((2, R, batches)),
            dma((2, Y, batches)),
            dma((2, R)),
            dma((2, Y)),
            dma((2, 2, hy, PARTS)),
            dma((2, R, Y)),
        ],
        compiler_params=pltpu.CompilerParams(
            collective_id=0, has_side_effects=True, vmem_limit_bytes=40 * 1024 * 1024
        ),
    )(grad_terms, acts, kept, starts)
    return result[None, None]


def solution(mesh, row=ROW):
    placed = (
        P("tensor", "dp", None),
        P("dp", "tensor"),
        P("dp", "tensor", None),
        P("tensor", None),
    )
    return jax.shard_map(
        functools.partial(shards, row, mesh.shape["tensor"]),
        mesh=mesh,
        in_specs=placed,
        out_specs=P("dp", "tensor", None, None, None),
        check_vma=False,
    )
```

time: 137 us -> 123 us (0.90)
  Pallas kernels: 132 us -> 118 us
    pallas_call x1, Pallas kernels: 132 us -> 118 us  [shards(): pl.pallas_call(functools.partial(body, Y, R, Z, NB), out_shape=jax.ShapeD...]
where the time goes in v3:
time: 123 us
  Pallas kernels  118 us (96%)
  local copies, waits for them, and re-layouts  5.17 us (4%)
    pallas_call x1, Pallas kernels, shards(): pl.pallas_call(functools.partial(body, Y, R, Z, NB), out_shape=jax.ShapeD...  118 us
    unnamed x9, local copies, waits for them, and re-layouts  5.17 us

profile of v3, /device:TPU:1, one launch (start us, length us, event | category | flops | bytes accessed | tf_op | source)
XLA Modules:
  0.0 123.2 jit_solution(16381959445441563701)
XLA Ops:
  0.0 0.0 copy-start
  0.0 1.9 %copy-done = bf16[1,128,12288]{2,1,0:T(8,128)(2,1)S(1)} copy-done((bf16[1,128,12288]{2,1,0:T(8,128)(2,1)S(1)}, bf16[1,128,12288]{2,1,0:T(8,128)(2,1)}, u32[]{:S(2)}) %copy-start) | copy-done | bytes 3145752
  1.9 0.0 copy-start.1
  1.9 1.0 copy-done.1
  2.9 0.0 copy-start.2
  2.9 0.7 copy-done.2
  3.5 0.0 copy-start.3
  3.5 0.7 copy-done.3
  4.2 118.0 %shard_map.46 = bf16[32,128,128]{2,1,0:T(8,128)(2,1)S(1)} custom-call(bf16[1,128,12288]{2,1,0:T(8,128)(2,1)S(1)} %copy-done, bf16[128,1536]{1,0:T(8,128)(2,1)S(1)} %copy-done.1, s32[1,1,32]{2,1,0:T(1,128)S(1)} %copy-done.2, s32[1,64]{1,0:T(1,128)S(1)} %copy-done.3), custom_call_target="tpu_custom_call" | custom-call | tf_op jit(solution)/shard_map/pallas_call | solution.py:460
  122.2 1.0 copy.6
Async XLA Ops:
  0.0 1.9 %copy-start = (bf16[1,128,12288]{2,1,0:T(8,128)(2,1)S(1)}, bf16[1,128,12288]{2,1,0:T(8,128)(2,1)}, u32[]{:S(2)}) copy-start(bf16[1,128,12288]{2,1,0:T(8,128)(2,1)} %grad.1) | copy-start | bytes 9437188
  1.9 1.0 copy-start.1
  2.9 0.7 copy-start.2
  3.5 0.7 copy-start.3

commit v4 on v3

--- a/solution.py
+++ b/solution.py
@@ -11,7 +11,7 @@
 POOL = 4
 ROW = 8
 SUBS = 4
-PARTS = 4
+PARTS = 2
 UNROLL = 8
 
 epsilon = 1e-06
@@ -51,6 +51,16 @@
     def y_dev(d):
         return (lax.rem(y + d + Y, Y) * R + s, t)
 
+    chips = Y * R // 2
+    chip, core = dp // 2, lax.rem(dp, 2)
+    twin = (2 * chip + 1 - core, t)
+
+    def chip_of(i):
+        return lax.rem(chip + i, chips)
+
+    def chip_dev(i):
+        return (2 * chip_of(i) + core, t)
+
     def send(src, dst, sems, index, device):
         copy = pltpu.make_async_remote_copy(
             src_ref=src, dst_ref=dst,
@@ -60,6 +70,10 @@
         copy.start()
         pending.append(copy)
 
+    def sent(copies):
+        for copy in copies:
+            copy.wait_send()
+
     def arrived(dst, sems, index, device):
         pltpu.make_async_remote_copy(
             src_ref=dst, dst_ref=dst,
@@ -75,10 +89,15 @@
         lax.fori_loop(0, n, one, 0, unroll=min(UNROLL, n))
 
     barrier = pltpu.get_barrier_semaphore()
-    partners = [z_dev(d) for d in range(1, Z)] + [row_dev(d) for d in range(1, R)]
-    partners += [y_dev(d) for d in range(1, Y)]
+    partners = [z_dev(d) for d in range(1, Z)] + [twin] + [row_dev(2 * d + 1 - 2 * core) for d in range(1, R // 2)]
     for device in partners:
         pl.semaphore_signal(barrier, inc=1, device_id=device, device_id_type=MESH)
+
+    def greet(i, _):
+        pl.semaphore_signal(barrier, inc=1, device_id=chip_dev(i), device_id_type=MESH)
+        return 0
+
+    lax.fori_loop(1, chips, greet, 0)
     inputs = [
         pltpu.make_async_copy(src, dst, in_sem.at[i])
         for i, (src, dst) in enumerate(((kept_in.at[0], kept), (kept_in.at[0], kept_s), (starts_in, starts), (acts_in, acts)))
@@ -88,13 +107,7 @@
     for i in range(Z):
         rows = pl.ds(pl.multiple_of(i * rz, rz), rz)
         pltpu.make_async_copy(grad.at[0, rows, :], own.at[rows, :], own_sem.at[i]).start()
-    inputs[0].wait()
-    mine[...] = jnp.full(mine.shape, -1, i32)
-    mine[0:1, 0:K] = kept[...]
-    pl.semaphore_wait(barrier, len(partners))
-
-    for d in range(1, Z):
-        send(mine, kz.at[d], kz_sem, (d,), z_dev(d))
+    pl.semaphore_wait(barrier, len(partners) + chips - 1)
 
     hz = Z // 2
     W = D // SUBS
@@ -123,7 +136,7 @@
                 q = firsts[1 - w][i]
                 z_send(w, 1, q, grad.at[0, z_rows((1 - 2 * w) * (hz - 1)), z_cols(q)])
 
-    for copy in inputs[1:]:
+    for copy in inputs[1:3]:
         copy.wait()
     ids = lax.broadcasted_iota(i32, tab.shape, 0) * BLOCK + lax.broadcasted_iota(i32, tab.shape, 1)
 
@@ -133,14 +146,11 @@
     mr[0] = lax.fori_loop(0, K, mark, jnp.zeros(tab.shape, i32), unroll=min(UNROLL, K))
     for d in range(1, R):
         send(mr.at[0], mr.at[d], mr_sem, (d,), row_dev(d))
-    for i in range(acts.shape[1] // BLOCK):
-        block = acts[:, i * BLOCK:(i + 1) * BLOCK].astype(f32)
-        acts_t[i] = block.T.astype(bf16)
-    to = lax.broadcasted_iota(i32, (BLOCK, BLOCK), 0)
-    frm = lax.broadcasted_iota(i32, (BLOCK, BLOCK), 1)
-    for i, (outer, inner) in enumerate(((R, KB), (KB, R))):
-        a, b, c = lax.div(to, inner * J), lax.rem(lax.div(to, J), inner), lax.rem(to, J)
-        perm[i] = jnp.where(frm == (b * outer + a) * J + c, 1.0, 0.0).astype(bf16)
+    inputs[0].wait()
+    mine[...] = jnp.full(mine.shape, -1, i32)
+    mine[0:1, 0:K] = kept[...]
+    for d in range(1, Z):
+        send(mine, kz.at[d], kz_sem, (d,), z_dev(d))
     for i in range(Z):
         rows = pl.ds(pl.multiple_of(i * rz, rz), rz)
         pltpu.make_async_copy(grad.at[0, rows, :], own.at[rows, :], own_sem.at[i]).wait()
@@ -159,13 +169,15 @@
         return m
 
     def marks_row():
+        my[0] = gathered(mr, mr_sem, row_dev, R)
+        for d in range(1, Y):
+            send(my.at[0], my.at[d], my_sem, (d,), y_dev(d))
+
+    def ranks():
         kz[0] = mine[...]
         for d in range(1, Z):
             arrived(kz.at[d], kz_sem, (d,), z_dev(-d))
         to_smem(kz, kz_s, 0)
-        my[0] = gathered(mr, mr_sem, row_dev, R)
-        for d in range(1, Y):
-            send(my.at[0], my.at[d], my_sem, (d,), y_dev(d))
 
     def places():
         m = gathered(my, my_sem, y_dev, Y)
@@ -217,6 +229,8 @@
         py[y] = gathered(pr, pr_sem, row_dev, R)
         for d in range(1, Y):
             send(py.at[y], py.at[y], py_sem, (d,), y_dev(d))
+
+    def going_back():
         square[...] = jnp.zeros(square.shape, f32)
         square[0:8, :] = py[y].astype(f32)
         turned = square[...].T
@@ -263,7 +277,7 @@
 
         loop(W // CH, add)
 
-    chores = [marks_row, places, places_row, places_all] + [functools.partial(select, b) for b in range(batches)] + [counts]
+    chores = {(1, SUBS - 1): marks_row, (2, 1): ranks, (2, SUBS - 1): places, (3, SUBS - 1): places_row}
     for j in range(1, hz):
         for i in range(SUBS):
             for w in range(2):
@@ -273,9 +287,9 @@
                 z_arrived(w, j - 1, q)
                 z_add(w, j - 1, q, (1 - 2 * w) * (hz - j))
                 z_send(w, j, q, zr.at[w, j - 1, :, z_cols(q)])
-            if chores and (i % 2 or j == hz - 1) and (j > 1 or i == SUBS - 1):
-                chores.pop(0)()
-    for chore in chores:
+            if (j, i) in chores:
+                chores.pop((j, i))()
+    for chore in chores.values():
         chore()
     mine_rows = z_rows(0)
     for q in range(SUBS):
@@ -295,6 +309,27 @@
         loop(W // CH, total_cols)
 
     far = sorted(range(1, Z), key=lambda d: -min(d, Z - d))
+
+    def set_up():
+        inputs[3].wait()
+        for i in range(acts.shape[1] // BLOCK):
+            block = acts[:, i * BLOCK:(i + 1) * BLOCK].astype(f32)
+            acts_t[i] = block.T.astype(bf16)
+        to = lax.broadcasted_iota(i32, (BLOCK, BLOCK), 0)
+        frm = lax.broadcasted_iota(i32, (BLOCK, BLOCK), 1)
+        for i, (outer, inner) in enumerate(((R, KB), (KB, R))):
+            a, b, c = lax.div(to, inner * J), lax.rem(lax.div(to, J), inner), lax.rem(to, J)
+            perm[i] = jnp.where(frm == (b * outer + a) * J + c, 1.0, 0.0).astype(bf16)
+
+    def selects():
+        places_all()
+        for b in range(batches):
+            select(b)
+        counts()
+
+    early = pending[:]
+    pending.clear()
+    chores = [set_up, going_back, selects, functools.partial(sent, early)]
     for b in range(batches):
         batch = pl.ds(b * KB, KB)
         for d in far:
@@ -310,6 +345,10 @@
             gsel[t, b * KB + i] = gsum[col]
 
         loop(KB, keep)
+        if chores:
+            chores.pop(0)()
+    for chore in chores:
+        chore()
 
     for b in range(batches):
         batch = pl.ds(b * KB, KB)
@@ -323,19 +362,29 @@
             tiles[:, i] = product.reshape(Y, RJ, BLOCK)
         for i in range(Y):
             turned = jnp.dot(perm[0], tiles[i].reshape(BLOCK, BLOCK), preferred_element_type=f32)
-            fwd[b, :, i] = turned.astype(bf16).reshape(R, H, BLOCK)
-        for d in range(1, R):
-            send(fwd.at[b, lax.rem(s + d, R)], mid.at[b, :, s], xa_sem, (d, b), row_dev(d))
-        mid[b, :, s] = fwd[b, s]
-        for d in range(1, R):
-            arrived(mid.at[b, :, lax.rem(s - d + R, R)], xa_sem, (d, b), row_dev(-d))
-        for d in sorted(range(1, Y), key=lambda d: -min(d, Y - d)):
-            send(mid.at[b, lax.rem(y + d, Y)], xs.at[b, y], ya_sem, (d, b), y_dev(d))
-        xs[b, y] = mid[b, y]
+            turned = turned.astype(bf16).reshape(R // 2, 2, H, BLOCK)
+            for c in range(2):
+                fwd[b, c, i] = turned[:, c]
+        send(fwd.at[b, 1 - core], mid.at[b, :, :, core], xa_sem, (b,), twin)
+        mid[b, :, :, core] = fwd[b, core]
+        arrived(mid.at[b, :, :, 1 - core], xa_sem, (b,), twin)
+
+        def direct(i, _):
+            to = chip_of(i)
+            pltpu.make_async_remote_copy(
+                src_ref=mid.at[b, to // (R // 2), lax.rem(to, R // 2)], dst_ref=xs.at[b, pl.ds(2 * chip, 2)],
+                send_sem=ya_sem.at[0, b], recv_sem=ya_sem.at[1, b],
+                device_id=chip_dev(i), device_id_type=MESH,
+            ).start()
+            return 0
+
+        lax.fori_loop(1, chips, direct, 0)
+        pltpu.make_async_copy(
+            mid.at[b, y, s // 2], xs.at[b, pl.ds(2 * chip, 2)], ya_sem.at[1, b]
+        ).start()
 
     for b in range(batches):
-        for d in range(1, Y):
-            arrived(xs.at[b, lax.rem(y - d + Y, Y)], ya_sem, (d, b), y_dev(-d))
+        arrived(xs.at[b], ya_sem, (b,), twin)
         here = jnp.dot(sel[b], xs[b].reshape(Y * BLOCK, BLOCK), preferred_element_type=f32)
         tot[...] = here if b == 0 else tot[...] + here
 
@@ -356,6 +405,7 @@
         if j == hy - 2 and h in firsts[w]:
             send(ag_part(-away * j, h), ag_part(-away * j, h), yag_sem, (w, hy - 1, h), y_dev(2 * away))
 
+    before = len(pending)
     full[y] = tot[...].astype(bf16)
     for i in range(PARTS):
         for w in range(2):
@@ -372,25 +422,29 @@
 
     near = sorted(range(1, R), key=lambda d: -min(d, R - d))
 
-    def give(d):
-        at = y_of(d)
-        rows = jnp.dot(back[...], full[at], preferred_element_type=f32).astype(bf16)
-        opack[at] = rows.reshape(batches, R, H, BLOCK)
+    groups = [(0,)] + [(d, -d) for d in range(1, hy - 1)] + [(hy - 1, 1 - hy, hy)]
+    begin = [0] + [2 * g - 1 for g in range(1, len(groups))]
+
+    def give(g):
+        for i, d in enumerate(groups[g]):
+            rows = jnp.dot(back[...], full[y_of(d)], preferred_element_type=f32).astype(bf16)
+            opack[begin[g] + i] = rows.reshape(batches, R, H, BLOCK)
+        at = pl.ds(begin[g], len(groups[g]))
         for e in near:
-            send(opack.at[at, :, lax.rem(s + e, R)], land.at[at, :, s], ret_sem, (e, d % Y), row_dev(e))
+            send(opack.at[at, :, lax.rem(s + e, R)], land.at[at, :, s], ret_sem, (e, g), row_dev(e))
         land[at, :, s] = opack[at, :, s]
 
-    def finish(d):
-        at = y_of(d)
+    def finish(g):
+        at = pl.ds(begin[g], len(groups[g]))
         for e in near:
-            arrived(land.at[at, :, lax.rem(s - e + R, R)], ret_sem, (e, d % Y), row_dev(-e))
-        rows = pl.ds(pl.multiple_of(at * RJ, RJ), RJ)
-        for b in range(batches):
-            turned = jnp.dot(perm[1], land[at, b].reshape(BLOCK, BLOCK), preferred_element_type=f32)
-            turned = turned.reshape(KB, RJ, BLOCK)
-            for i in range(KB):
-                k = b * KB + i
-                out[k, rows, :] = (turned[i] * facs[k:k + 1, :]).astype(bf16)
+            arrived(land.at[at, :, lax.rem(s - e + R, R)], ret_sem, (e, g), row_dev(-e))
+        for i, d in enumerate(groups[g]):
+            rows = pl.ds(pl.multiple_of(y_of(d) * RJ, RJ), RJ)
+            for b in range(batches):
+                turned = jnp.dot(perm[1], land[begin[g] + i, b].reshape(BLOCK, BLOCK), preferred_element_type=f32)
+                turned = turned.reshape(KB, RJ, BLOCK)
+                for k in range(KB):
+                    out[b * KB + k, rows, :] = (turned[k] * facs[b * KB + k:b * KB + k + 1, :]).astype(bf16)
 
     def energies(ref, sems, dev, n):
         sum_ = ref[0]
@@ -414,33 +468,43 @@
 
         loop(K, one)
 
-    give(0)
-    energy_row()
-    waiting = [0]
-    for j in range(1, hy + 1):
+    def ag_come(j):
+        hop = 2 if j == hy else 1
         for i in range(PARTS):
             for w in range(2):
                 h = i if w == 0 else PARTS - 1 - i
-                if j == hy and h not in firsts[w]:
-                    continue
-                hop = 2 if j == hy else 1
-                arrived(ag_part(-(1 - 2 * w) * j, h), yag_sem, (w, j - 1, h), y_dev(-(1 - 2 * w) * hop))
-                if j < hy:
+                if j < hy or h in firsts[w]:
+                    away = 1 - 2 * w
+                    arrived(ag_part(-away * j, h), yag_sem, (w, j - 1, h), y_dev(-away * hop))
                     ag_send(w, j, h)
-        come = (-j, j) if j < hy else (j,)
-        for d in come:
-            give(d)
-        if j == 2:
-            factors()
-        if j > 2:
-            for d in waiting[:2]:
-                finish(d)
-            waiting = waiting[2:]
-        waiting += come
-    for d in waiting:
-        finish(d)
-    for copy in pending:
-        copy.wait_send()
+
+    last = len(groups) - 1
+    forward = pending[:before]
+    del pending[:before]
+    give(0)
+    for j in range(1, last):
+        ag_come(j)
+        if j == 1:
+            energy_row()
+        give(j)
+    if last == 1:
+        energy_row()
+    factors()
+    sent(forward)
+    for g in range(last - 1):
+        finish(g)
+    ag_come(hy - 1)
+    ag_come(hy)
+    give(last)
+    finish(last - 1)
+    for b in range(batches):
+        some = xs.at[b, pl.ds(0, 2 * chips - 2)]
+        pltpu.make_async_remote_copy(
+            src_ref=some, dst_ref=some, send_sem=ya_sem.at[0, b], recv_sem=ya_sem.at[1, b],
+            device_id=twin, device_id_type=MESH,
+        ).wait_send()
+    sent(pending)
+    finish(last)
 
 
 def shards(R, Z, grad_terms, acts, kept, starts):
@@ -475,9 +539,9 @@
             vmem((acts.shape[1] // BLOCK, BLOCK, BLOCK), bf16),
             vmem((2, BLOCK, BLOCK), bf16),
             vmem((Y, Y, R * J, BLOCK), bf16),
-            vmem((batches, R, Y, H, BLOCK), bf16),
-            vmem((batches, Y, R, H, BLOCK), bf16),
-            vmem((batches, Y, R, H, BLOCK), bf16),
+            vmem((batches, 2, Y, R // 2, H, BLOCK), bf16),
+            vmem((batches, Y, R // 2, 2, H, BLOCK), bf16),
+            vmem((batches, Y * R, H, BLOCK), bf16),
             vmem((batches, SR, Y * BLOCK), bf16),
             vmem((SR, BLOCK), f32),
             vmem((BLOCK, BLOCK), f32),
@@ -511,15 +575,15 @@
             dma((4,)),
             dma((2, 2, hz, SUBS)),
             dma((2, Z, batches)),
-            dma((2, R, batches)),
-            dma((2, Y, batches)),
+            dma((2, batches)),
+            dma((2, batches)),
             dma((2, R)),
             dma((2, Y)),
             dma((2, 2, hy, PARTS)),
-            dma((2, R, Y)),
+            dma((2, R, hy)),
         ],
         compiler_params=pltpu.CompilerParams(
-            collective_id=0, has_side_effects=True, vmem_limit_bytes=40 * 1024 * 1024
+            collective_id=0, has_side_effects=True, vmem_limit_bytes=56 * 1024 * 1024
         ),
     )(grad_terms, acts, kept, starts)
     return result[None, None]

time: 123 us -> 116 us (0.943)
  Pallas kernels: 118 us -> 114 us
  local copies, waits for them, and re-layouts: 5.17 us -> 2.31 us
    pallas_call x1, Pallas kernels: 118 us -> 114 us  [shards(): pl.pallas_call(functools.partial(body, Y, R, Z, NB), out_shape=jax.ShapeD...]
    unnamed x9 -> x1, local copies, waits for them, and re-layouts: 5.17 us -> 2.31 us
where the time goes in v4:
time: 116 us
  Pallas kernels  114 us (98%)
  local copies, waits for them, and re-layouts  2.31 us (2%)
    pallas_call x1, Pallas kernels, shards(): pl.pallas_call(functools.partial(body, Y, R, Z, NB), out_shape=jax.ShapeD...  114 us

profile of v4, /device:TPU:1, one launch (start us, length us, event | category | flops | bytes accessed | tf_op | source)
XLA Modules:
  0.0 115.9 jit_solution(12440287629234287649)
XLA Ops:
  0.0 113.6 %shard_map.46 = bf16[32,128,128]{2,1,0:T(8,128)(2,1)} custom-call(bf16[1,128,12288]{2,1,0:T(8,128)(2,1)} %grad.1, bf16[128,1536]{1,0:T(8,128)(2,1)} %acts_in.1, s32[1,1,32]{2,1,0:T(1,128)} %kept_in.1, s32[1,64]{1,0:T(1,128)} %starts_in.1), custom_call_target="tpu_custom_call" | custom-call | tf_op jit(solution)/shard_map/pallas_call | solution.py:524
  113.6 2.3 %copy.6 = bf16[1,1,32,128,128]{4,3,2,1,0:T(8,128)(2,1)} copy(bf16[1,1,32,128,128]{4,3,2,1,0:T(8,128)(2,1)} %bitcast.1) | data formatting | bytes 2097152

commit v5 on v4

--- a/solution.py
+++ b/solution.py
@@ -11,7 +11,7 @@
 POOL = 4
 ROW = 8
 SUBS = 4
-PARTS = 2
+PARTS = 4
 UNROLL = 8
 
 epsilon = 1e-06
@@ -23,10 +23,10 @@
     Y, R, Z, NB,
     grad, acts_in, kept_in, starts_in, out,
     acts, kept, kept_s, starts, own, zr, gsum, pack, gsel, acts_t, perm, tiles, fwd, mid, xs, sel, tot,
-    esq, eb, ey, fac, facs, full, back, opack, land, mine, kz, mr, my, pr, py, tab, square,
+    esq, eb, ey, fac, facs, full, back, opack, ostraight, land, mine, kz, mr, my, pr, py, tab, square,
     kz_s, c_s, p_s, fac_s,
     in_sem, own_sem, kz_sem, mr_sem, my_sem, pr_sem, py_sem, loc_sem, zrs_sem, za_sem, xa_sem, ya_sem,
-    er_sem, ey_sem, yag_sem, ret_sem,
+    er_sem, ey_sem, yag_sem, ret_sem, straight_sem,
 ):
     dp, t = lax.axis_index("dp"), lax.axis_index("tensor")
     y, s = dp // R, lax.rem(dp, R)
@@ -89,15 +89,15 @@
         lax.fori_loop(0, n, one, 0, unroll=min(UNROLL, n))
 
     barrier = pltpu.get_barrier_semaphore()
-    partners = [z_dev(d) for d in range(1, Z)] + [twin] + [row_dev(2 * d + 1 - 2 * core) for d in range(1, R // 2)]
+    partners = [z_dev(d) for d in range(1, Z)]
     for device in partners:
         pl.semaphore_signal(barrier, inc=1, device_id=device, device_id_type=MESH)
 
     def greet(i, _):
-        pl.semaphore_signal(barrier, inc=1, device_id=chip_dev(i), device_id_type=MESH)
+        pl.semaphore_signal(barrier, inc=1, device_id=(lax.rem(dp + i, Y * R), t), device_id_type=MESH)
         return 0
 
-    lax.fori_loop(1, chips, greet, 0)
+    lax.fori_loop(1, Y * R, greet, 0)
     inputs = [
         pltpu.make_async_copy(src, dst, in_sem.at[i])
         for i, (src, dst) in enumerate(((kept_in.at[0], kept), (kept_in.at[0], kept_s), (starts_in, starts), (acts_in, acts)))
@@ -107,7 +107,7 @@
     for i in range(Z):
         rows = pl.ds(pl.multiple_of(i * rz, rz), rz)
         pltpu.make_async_copy(grad.at[0, rows, :], own.at[rows, :], own_sem.at[i]).start()
-    pl.semaphore_wait(barrier, len(partners) + chips - 1)
+    pl.semaphore_wait(barrier, len(partners) + Y * R - 1)
 
     hz = Z // 2
     W = D // SUBS
@@ -230,13 +230,19 @@
         for d in range(1, Y):
             send(py.at[y], py.at[y], py_sem, (d,), y_dev(d))
 
+    half0 = range(batches // 2)
+    halves = (half0, range(len(half0), batches))
+    ways = [(0, range(batches)), (1, range(batches)), (2, halves[0]), (-1, range(batches)), (-2, halves[1])]
+
     def going_back():
+        lane = lax.broadcasted_iota(i32, (BLOCK, SR), 1).astype(f32)
         square[...] = jnp.zeros(square.shape, f32)
-        square[0:8, :] = py[y].astype(f32)
-        turned = square[...].T
-        lane = lax.broadcasted_iota(i32, (BLOCK, SR), 1).astype(f32)
-        for b in range(batches):
-            back[b * BLOCK:(b + 1) * BLOCK, :] = jnp.where(turned[:, b:b + 1] == lane, 1.0, 0.0).astype(bf16)
+        for i, (away, parts) in enumerate(ways):
+            square[0:8, :] = py[lax.rem(y + away + Y, Y)].astype(f32)
+            turned = square[...].T
+            for b in parts:
+                rows = jnp.where(turned[:, b:b + 1] == lane, 1.0, 0.0).astype(bf16)
+                back[i, b * BLOCK:(b + 1) * BLOCK, :] = rows
 
     def places_all():
         for d in range(1, Y):
@@ -292,7 +298,7 @@
     for chore in chores.values():
         chore()
     mine_rows = z_rows(0)
-    for q in range(SUBS):
+    for q in [q for pair in zip(*firsts) for q in pair]:
         for w in range(2):
             if hz > 1 or q in firsts[w]:
                 z_arrived(w, hz - 1, q)
@@ -329,7 +335,7 @@
 
     early = pending[:]
     pending.clear()
-    chores = [set_up, going_back, selects, functools.partial(sent, early)]
+    chores = [set_up, selects, going_back, functools.partial(sent, early)]
     for b in range(batches):
         batch = pl.ds(b * KB, KB)
         for d in far:
@@ -399,11 +405,9 @@
         return full.at[y_of(d), pl.ds(h * HS, HS)]
 
     def ag_send(w, j, h):
-        away = 1 - 2 * w
-        if j < hy - 1:
+        if j < hy - 2:
+            away = 1 - 2 * w
             send(ag_part(-away * j, h), ag_part(-away * j, h), yag_sem, (w, j, h), y_dev(away))
-        if j == hy - 2 and h in firsts[w]:
-            send(ag_part(-away * j, h), ag_part(-away * j, h), yag_sem, (w, hy - 1, h), y_dev(2 * away))
 
     before = len(pending)
     full[y] = tot[...].astype(bf16)
@@ -424,27 +428,63 @@
 
     groups = [(0,)] + [(d, -d) for d in range(1, hy - 1)] + [(hy - 1, 1 - hy, hy)]
     begin = [0] + [2 * g - 1 for g in range(1, len(groups))]
+    last = len(groups) - 1
 
     def give(g):
         for i, d in enumerate(groups[g]):
-            rows = jnp.dot(back[...], full[y_of(d)], preferred_element_type=f32).astype(bf16)
+            rows = jnp.dot(back[0], full[y_of(d)], preferred_element_type=f32).astype(bf16)
             opack[begin[g] + i] = rows.reshape(batches, R, H, BLOCK)
         at = pl.ds(begin[g], len(groups[g]))
         for e in near:
             send(opack.at[at, :, lax.rem(s + e, R)], land.at[at, :, s], ret_sem, (e, g), row_dev(e))
         land[at, :, s] = opack[at, :, s]
 
+    def way(w, hop):
+        i = 2 * w + hop
+        parts = ways[i][1]
+        return i, hop * (1 - 2 * w), pl.ds(parts[0], len(parts)), begin[last] + (2 if hop == 2 else 1 - w)
+
+    both = [(w, hop) for hop in (1, 2) for w in range(2) if len(ways[2 * w + hop][1])]
+
+    def straight():
+        for w, hop in both:
+            i, away, parts, at = way(w, hop)
+            chunk = full[y_of(-(1 - 2 * w) * (hy - 2))]
+            rows = jnp.dot(
+                back[i, pl.ds(parts.start * BLOCK, parts.size * BLOCK), :], chunk, preferred_element_type=f32
+            )
+            ostraight[i - 1, parts] = rows.astype(bf16).reshape(parts.size, R, H, BLOCK)
+            for e in range(R):
+                to = lax.rem(s + e, R)
+                send(
+                    ostraight.at[i - 1, parts, to], land.at[at, parts, s], straight_sem, (i - 1, e),
+                    (y_of(away) * R + to, t),
+                )
+
+    def place_rows(at, d):
+        rows = pl.ds(pl.multiple_of(y_of(d) * RJ, RJ), RJ)
+        for b in range(batches):
+            turned = jnp.dot(perm[1], land[at, b].reshape(BLOCK, BLOCK), preferred_element_type=f32)
+            turned = turned.reshape(KB, RJ, BLOCK)
+            for k in range(KB):
+                out[b * KB + k, rows, :] = (turned[k] * facs[b * KB + k:b * KB + k + 1, :]).astype(bf16)
+
     def finish(g):
         at = pl.ds(begin[g], len(groups[g]))
         for e in near:
             arrived(land.at[at, :, lax.rem(s - e + R, R)], ret_sem, (e, g), row_dev(-e))
         for i, d in enumerate(groups[g]):
-            rows = pl.ds(pl.multiple_of(y_of(d) * RJ, RJ), RJ)
-            for b in range(batches):
-                turned = jnp.dot(perm[1], land[begin[g] + i, b].reshape(BLOCK, BLOCK), preferred_element_type=f32)
-                turned = turned.reshape(KB, RJ, BLOCK)
-                for k in range(KB):
-                    out[b * KB + k, rows, :] = (turned[k] * facs[b * KB + k:b * KB + k + 1, :]).astype(bf16)
+            place_rows(begin[g] + i, d)
+
+    def finish_straight():
+        for w, hop in both:
+            i, away, parts, at = way(w, hop)
+            for e in range(R):
+                come = lax.rem(s - e + R, R)
+                arrived(land.at[at, parts, come], straight_sem, (i - 1, e), (y_of(-away) * R + come, t))
+            if hop == 1:
+                place_rows(at, groups[last][1 - w])
+        place_rows(begin[last] + 2, hy)
 
     def energies(ref, sems, dev, n):
         sum_ = ref[0]
@@ -469,16 +509,13 @@
         loop(K, one)
 
     def ag_come(j):
-        hop = 2 if j == hy else 1
         for i in range(PARTS):
             for w in range(2):
                 h = i if w == 0 else PARTS - 1 - i
-                if j < hy or h in firsts[w]:
-                    away = 1 - 2 * w
-                    arrived(ag_part(-away * j, h), yag_sem, (w, j - 1, h), y_dev(-away * hop))
-                    ag_send(w, j, h)
-
-    last = len(groups) - 1
+                away = 1 - 2 * w
+                arrived(ag_part(-away * j, h), yag_sem, (w, j - 1, h), y_dev(-away))
+                ag_send(w, j, h)
+
     forward = pending[:before]
     del pending[:before]
     give(0)
@@ -486,17 +523,16 @@
         ag_come(j)
         if j == 1:
             energy_row()
+        if j == last - 1:
+            straight()
         give(j)
     if last == 1:
+        straight()
         energy_row()
     factors()
     sent(forward)
-    for g in range(last - 1):
+    for g in range(last):
         finish(g)
-    ag_come(hy - 1)
-    ag_come(hy)
-    give(last)
-    finish(last - 1)
     for b in range(batches):
         some = xs.at[b, pl.ds(0, 2 * chips - 2)]
         pltpu.make_async_remote_copy(
@@ -504,7 +540,7 @@
             device_id=twin, device_id_type=MESH,
         ).wait_send()
     sent(pending)
-    finish(last)
+    finish_straight()
 
 
 def shards(R, Z, grad_terms, acts, kept, starts):
@@ -550,8 +586,9 @@
             vmem((8, BLOCK), f32),
             vmem((K, BLOCK), f32),
             vmem((Y, SR, BLOCK), bf16),
-            vmem((batches * BLOCK, SR), bf16),
+            vmem((5, batches * BLOCK, SR), bf16),
             vmem((Y, batches, R, H, BLOCK), bf16),
+            vmem((4, batches, R, H, BLOCK), bf16),
             vmem((Y, batches, R, H, BLOCK), bf16),
             vmem((8, BLOCK), i32),
             vmem((Z, 8, BLOCK), i32),
@@ -581,6 +618,7 @@
             dma((2, Y)),
             dma((2, 2, hy, PARTS)),
             dma((2, R, hy)),
+            dma((2, 4, R)),
         ],
         compiler_params=pltpu.CompilerParams(
             collective_id=0, has_side_effects=True, vmem_limit_bytes=56 * 1024 * 1024

time: 116 us -> 114 us (0.983)
  Pallas kernels: 114 us -> 112 us
    pallas_call x1, Pallas kernels: 114 us -> 112 us  [shards(): pl.pallas_call(functools.partial(body, Y, R, Z, NB), out_shape=jax.ShapeD...]
where the time goes in v5:
time: 114 us
  Pallas kernels  112 us (98%)
  local copies, waits for them, and re-layouts  2.31 us (2%)
    pallas_call x1, Pallas kernels, shards(): pl.pallas_call(functools.partial(body, Y, R, Z, NB), out_shape=jax.ShapeD...  112 us
    unnamed x1, local copies, waits for them, and re-layouts  2.31 us

profile of v5, /device:TPU:1, one launch (start us, length us, event | category | flops | bytes accessed | tf_op | source)
XLA Modules:
  0.0 114.2 jit_solution(12755259651498082703)
XLA Ops:
  0.0 111.8 %shard_map.46 = bf16[32,128,128]{2,1,0:T(8,128)(2,1)} custom-call(bf16[1,128,12288]{2,1,0:T(8,128)(2,1)} %grad.1, bf16[128,1536]{1,0:T(8,128)(2,1)} %acts_in.1, s32[1,1,32]{2,1,0:T(1,128)} %kept_in.1, s32[1,64]{1,0:T(1,128)} %starts_in.1), custom_call_target="tpu_custom_call" | custom-call | tf_op jit(solution)/shard_map/pallas_call | solution.py:560
  111.8 2.3 %copy.6 = bf16[1,1,32,128,128]{4,3,2,1,0:T(8,128)(2,1)} copy(bf16[1,1,32,128,128]{4,3,2,1,0:T(8,128)(2,1)} %bitcast.1) | data formatting | bytes 2097152
